TPU v7x, 32 devices: a whole 2x2x4 slice. The times are simulated.
32 devices in a mesh: ctx: 8 (over y, x, core), fsdp: 4 (over z).
Axes of the slice: x: 2, y: 2, z: 4, core: 2. Of those that a mesh axis runs over, the one named last changes fastest.
Arguments:
- hidden_in: bfloat16 [2, 8, 1024, 1024], P(None, 'fsdp', 'ctx'), may hold values from -6 to 6
- lengths: int32 [2, 8], P(None, 'fsdp'), may hold values from 256 to 1024, as said below
- cotangent: bfloat16 [2, 8, 1024, 1024], P(None, 'fsdp', 'ctx'), may hold values from -6 to 6
- w_qkv: bfloat16 [1024, 3072], P('fsdp'), may hold values from -0.1875 to 0.1875
- bias_q: bfloat16 [1024], P('fsdp'), may hold values from -3 to 3
- bias_v: bfloat16 [1024], P('fsdp'), may hold values from -0.1875 to 0.1875
- w_out: bfloat16 [1024, 1024], P('fsdp'), may hold values from -4 to 4
- bias_out: bfloat16 [1024], P('fsdp'), may hold values from -2 to 2
- ln1_gain: bfloat16 [1024], P('fsdp'), may hold values from 0.25 to 1.75
- ln1_bias: bfloat16 [1024], P('fsdp'), may hold values from -2 to 2
- w_up: bfloat16 [1024, 4096], P('fsdp'), may hold values from -0.1875 to 0.1875
- bias_up: bfloat16 [4096], P('fsdp'), may hold values from -3 to 3
- w_down: bfloat16 [4096, 1024], P('fsdp'), may hold values from -0.09375 to 0.09375
- bias_down: bfloat16 [1024], P('fsdp'), may hold values from -2 to 2
- ln2_gain: bfloat16 [1024], P('fsdp'), may hold values from 0.25 to 1.75
- ln2_bias: bfloat16 [1024], P('fsdp'), may hold values from -2 to 2
Outputs:
- out_hidden: bfloat16 [2, 8, 1024, 1024], P(None, 'fsdp', 'ctx')
- grad_hidden: float32 [2, 8, 1024, 1024], P(None, 'fsdp', 'ctx')
- grad_w_qkv: float32 [1024, 3072], P('fsdp')
- grad_bias_q: float32 [1024], P('fsdp')
- grad_bias_v: float32 [1024], P('fsdp')
- grad_w_out: float32 [1024, 1024], P('fsdp')
- grad_bias_out: float32 [1024], P('fsdp')
- grad_ln1_gain: float32 [1024], P('fsdp')
- grad_ln1_bias: float32 [1024], P('fsdp')
- grad_w_up: float32 [1024, 4096], P('fsdp')
- grad_bias_up: float32 [4096], P('fsdp')
- grad_w_down: float32 [4096, 1024], P('fsdp')
- grad_bias_down: float32 [1024], P('fsdp')
- grad_ln2_gain: float32 [1024], P('fsdp')
- grad_ln2_bias: float32 [1024], P('fsdp')
Inputs may be any that keep to these rules, and one draw needn't show every extreme that they name: `lengths`: in every micro-batch, one of the 2 sequences of each index of fsdp, chosen by the seed, fills all 1024 slots.
All inputs are finite; a program needn't handle non-finite values.
Results may differ from a plain program's by a relative error of at most 0.025.
Values may be sent and summed in bfloat16 or wider, within the bound.
A program may use at most 384 MiB of HBM per device.

v0:
```python
import jax
import jax.numpy as jnp
from jax import lax
from jax.sharding import PartitionSpec as P

HEADS = 16
HEAD_DIM = 64


EPS = 1e-05
NEG_FILL = -1e30


def as_sent(value):

    def short(part):
        return part.astype(jnp.bfloat16) if part.dtype == jnp.float32 else part

    return jax.tree.map(short, value)


def layer_norm(inputs, ln_gain, ln_shift):
    center = jnp.mean(inputs, axis=-1, keepdims=True)
    centered = inputs - center
    spread = jnp.mean(centered * centered, axis=-1, keepdims=True)
    return centered * lax.rsqrt(spread + EPS) * ln_gain + ln_shift


def exact_gelu(inputs):
    return jax.nn.gelu(inputs, approximate=False)


def allowed_mask(seq_lengths, query_pos, key_pos):
    causal = key_pos[None, :] <= query_pos[:, None]
    within = key_pos[None, None, :] < seq_lengths[:, None, None]
    return (causal[None] & within)[:, None]


def rows_sum(matrix):
    return jnp.sum(matrix.astype(jnp.float32), axis=0)


def matmul(left_side, right_side):
    return jnp.dot(left_side, right_side, preferred_element_type=jnp.float32)


def body(
    hidden_in,
    lengths,
    cotangent,
    w_qkv,
    bias_q,
    bias_v,
    w_out,
    bias_out,
    ln1_gain,
    ln1_bias,
    w_up,
    bias_up,
    w_down,
    bias_down,
    ln2_gain,
    ln2_bias,
):
    shards = (
        w_qkv,
        bias_q,
        bias_v,
        w_out,
        bias_out,
        ln1_gain,
        ln1_bias,
        w_up,
        bias_up,
        w_down,
        bias_down,
        ln2_gain,
        ln2_bias,
    )
    batch_count, seq_count, slot_dev, model_width = hidden_in.shape
    head_count = HEADS
    head_width = HEAD_DIM
    row_count = seq_count * slot_dev
    scale_factor = head_width ** (-0.5)
    query_pos = lax.axis_index("ctx") * slot_dev + jnp.arange(slot_dev, dtype=jnp.int32)
    grad_totals = None
    out_list = []
    grad_list = []
    for micro in range(batch_count):
        seq_lengths = lengths[micro]
        gathered = (
            lax.all_gather(shards[0], "fsdp", axis=0, tiled=True),
            lax.all_gather(shards[1], "fsdp", axis=0, tiled=True),
            lax.all_gather(shards[2], "fsdp", axis=0, tiled=True),
            lax.all_gather(shards[3], "fsdp", axis=0, tiled=True),
            lax.all_gather(shards[4], "fsdp", axis=0, tiled=True),
            lax.all_gather(shards[5], "fsdp", axis=0, tiled=True),
            lax.all_gather(shards[6], "fsdp", axis=0, tiled=True),
            lax.all_gather(shards[7], "fsdp", axis=0, tiled=True),
            lax.all_gather(shards[8], "fsdp", axis=0, tiled=True),
            lax.all_gather(shards[9], "fsdp", axis=0, tiled=True),
            lax.all_gather(shards[10], "fsdp", axis=0, tiled=True),
            lax.all_gather(shards[11], "fsdp", axis=0, tiled=True),
            lax.all_gather(shards[12], "fsdp", axis=0, tiled=True),
        )
        (
            full_qkv,
            full_bias_q,
            full_bias_v,
            full_out,
            full_bias_out,
            full_g1,
            full_c1,
            full_up,
            full_bias_up,
            full_down,
            full_bias_down,
            full_g2,
            full_c2,
        ) = gathered
        gain_one = full_g1.astype(jnp.float32)
        shift_one = full_c1.astype(jnp.float32)
        gain_two = full_g2.astype(jnp.float32)
        shift_two = full_c2.astype(jnp.float32)
        flat_in = hidden_in[micro].reshape(row_count, model_width).astype(jnp.float32)
        normed = layer_norm(flat_in, gain_one, shift_one).astype(jnp.bfloat16)
        projected = matmul(normed, full_qkv)
        query_rows = (projected[:, :model_width] + full_bias_q).astype(jnp.bfloat16)
        key_rows = projected[:, model_width : 2 * model_width].astype(jnp.bfloat16)
        value_rows = (projected[:, 2 * model_width :] + full_bias_v).astype(jnp.bfloat16)
        queries = query_rows.reshape(seq_count, slot_dev, head_count, head_width)
        kv_pack = jnp.concatenate([key_rows, value_rows], axis=1).reshape(
            seq_count, slot_dev, 2 * model_width
        )
        portion = lax.all_gather(kv_pack, "ctx", axis=1, tiled=True)
        run_max = jnp.full((seq_count, head_count, slot_dev), NEG_FILL, jnp.float32)
        rows = portion.shape[1]
        keys_here = portion[:, :, :model_width].reshape(seq_count, rows, head_count, head_width)
        values_here = portion[:, :, model_width:].reshape(seq_count, rows, head_count, head_width)
        key_pos = jnp.arange(rows, dtype=jnp.int32)
        allowed = allowed_mask(seq_lengths, query_pos, key_pos)
        scores = (
            jnp.einsum("sqhe,skhe->shqk", queries, keys_here, preferred_element_type=jnp.float32)
            * scale_factor
        )
        masked = jnp.where(allowed, scores, NEG_FILL)
        new_max = jnp.maximum(run_max, jnp.max(masked, axis=-1))
        weights = jnp.where(allowed, jnp.exp(masked - new_max[..., None]), 0.0)
        new_total = jnp.sum(weights, axis=-1)
        update = jnp.einsum(
            "shqk,skhe->shqe",
            weights.astype(jnp.bfloat16),
            values_here,
            preferred_element_type=jnp.float32,
        )
        row_max = new_max
        mixed_heads = update / new_total[..., None]
        mixed_low = (
            jnp.transpose(mixed_heads, (0, 2, 1, 3))
            .reshape(row_count, model_width)
            .astype(jnp.bfloat16)
        )
        residual = flat_in + matmul(mixed_low, full_out) + full_bias_out
        normed2 = layer_norm(residual, gain_two, shift_two).astype(jnp.bfloat16)
        pre_act = matmul(normed2, full_up) + full_bias_up
        activated = exact_gelu(pre_act).astype(jnp.bfloat16)
        output = residual + matmul(activated, full_down) + full_bias_down
        out_list.append(output.astype(jnp.bfloat16).reshape(seq_count, slot_dev, model_width))
        back_params = (
            lax.all_gather(shards[0], "fsdp", axis=0, tiled=True),
            lax.all_gather(shards[1], "fsdp", axis=0, tiled=True),
            lax.all_gather(shards[2], "fsdp", axis=0, tiled=True),
            lax.all_gather(shards[3], "fsdp", axis=0, tiled=True),
            lax.all_gather(shards[4], "fsdp", axis=0, tiled=True),
            lax.all_gather(shards[5], "fsdp", axis=0, tiled=True),
            lax.all_gather(shards[6], "fsdp", axis=0, tiled=True),
            lax.all_gather(shards[7], "fsdp", axis=0, tiled=True),
            lax.all_gather(shards[8], "fsdp", axis=0, tiled=True),
            lax.all_gather(shards[9], "fsdp", axis=0, tiled=True),
            lax.all_gather(shards[10], "fsdp", axis=0, tiled=True),
            lax.all_gather(shards[11], "fsdp", axis=0, tiled=True),
            lax.all_gather(shards[12], "fsdp", axis=0, tiled=True),
        )
        back_qkv = back_params[0]
        back_out = back_params[3]
        back_up = back_params[7]
        back_down = back_params[9]
        query_filled = (
            (query_pos[None, :] < seq_lengths[:, None]).astype(jnp.float32).reshape(row_count, 1)
        )
        d_out = cotangent[micro].reshape(row_count, model_width).astype(jnp.float32) * query_filled
        d_branch = d_out.astype(jnp.bfloat16)
        grad_w_down = matmul(activated.T, d_branch)
        grad_bias_down = jnp.sum(d_out, axis=0)
        d_activ = matmul(d_branch, back_down.T)
        gelu_pull = jax.vjp(exact_gelu, pre_act)[1]
        d_pre = gelu_pull(d_activ)[0].astype(jnp.bfloat16)
        grad_w_up = matmul(normed2.T, d_pre)
        grad_bias_up = rows_sum(d_pre)
        d_normed2 = matmul(d_pre, back_up.T)
        norm_pull_two = jax.vjp(layer_norm, residual, gain_two, shift_two)[1]
        d_resid_norm, grad_ln2_gain, grad_ln2_bias = norm_pull_two(d_normed2)
        d_residual = d_out + d_resid_norm
        d_attn = d_residual.astype(jnp.bfloat16)
        grad_w_out = matmul(mixed_low.T, d_attn)
        grad_bias_out = rows_sum(d_attn)
        d_mixed = jnp.transpose(
            matmul(d_attn, back_out.T).reshape(seq_count, slot_dev, head_count, head_width),
            (0, 2, 1, 3),
        )
        d_numer = (d_mixed / new_total[..., None]).astype(jnp.bfloat16)
        d_total = -jnp.sum(d_mixed * mixed_heads, axis=-1) / new_total

        def key_back(portion):
            rows = portion.shape[1]
            keys_here = portion[:, :, :model_width].reshape(seq_count, rows, head_count, head_width)
            values_here = portion[:, :, model_width:].reshape(
                seq_count, rows, head_count, head_width
            )
            key_pos = jnp.arange(rows, dtype=jnp.int32)
            allowed = allowed_mask(seq_lengths, query_pos, key_pos)
            scores = (
                jnp.einsum(
                    "sqhe,skhe->shqk", queries, keys_here, preferred_element_type=jnp.float32
                )
                * scale_factor
            )
            masked = jnp.where(allowed, scores, NEG_FILL)
            weights = jnp.where(allowed, jnp.exp(masked - row_max[..., None]), 0.0)
            d_value = jnp.einsum(
                "shqk,shqe->skhe",
                weights.astype(jnp.bfloat16),
                d_numer,
                preferred_element_type=jnp.float32,
            )
            d_weight = (
                jnp.einsum(
                    "shqe,skhe->shqk", d_numer, values_here, preferred_element_type=jnp.float32
                )
                + d_total[..., None]
            )
            d_score = (weights * d_weight).astype(jnp.bfloat16)
            d_query = (
                jnp.einsum(
                    "shqk,skhe->sqhe", d_score, keys_here, preferred_element_type=jnp.float32
                )
                * scale_factor
            )
            d_key = (
                jnp.einsum("shqk,sqhe->skhe", d_score, queries, preferred_element_type=jnp.float32)
                * scale_factor
            )
            term = jnp.concatenate(
                [
                    d_key.reshape(seq_count, rows, model_width),
                    d_value.reshape(seq_count, rows, model_width),
                ],
                axis=2,
            )
            return (d_query, term)

        d_query, d_keys_all = key_back(lax.all_gather(kv_pack, "ctx", axis=1, tiled=True))
        d_keys_mine = lax.psum_scatter(
            d_keys_all.astype(jnp.bfloat16), "ctx", scatter_dimension=1, tiled=True
        ).astype(jnp.float32)
        d_key_rows = d_keys_mine[:, :, :model_width].reshape(row_count, model_width)
        d_value_rows = d_keys_mine[:, :, model_width:].reshape(row_count, model_width)
        d_qkv = jnp.concatenate(
            [d_query.reshape(row_count, model_width), d_key_rows, d_value_rows], axis=1
        ).astype(jnp.bfloat16)
        grad_w_qkv = matmul(normed.T, d_qkv)
        grad_bias_q = rows_sum(d_qkv[:, :model_width])
        grad_bias_v = rows_sum(d_qkv[:, 2 * model_width :])
        d_normed = matmul(d_qkv, back_qkv.T)
        norm_pull_one = jax.vjp(layer_norm, flat_in, gain_one, shift_one)[1]
        d_input_norm, grad_ln1_gain, grad_ln1_bias = norm_pull_one(d_normed)
        grad_list.append((d_residual + d_input_norm).reshape(seq_count, slot_dev, model_width))
        step_grads = (
            grad_w_qkv,
            grad_bias_q,
            grad_bias_v,
            grad_w_out,
            grad_bias_out,
            grad_ln1_gain,
            grad_ln1_bias,
            grad_w_up,
            grad_bias_up,
            grad_w_down,
            grad_bias_down,
            grad_ln2_gain,
            grad_ln2_bias,
        )
        if grad_totals is None:
            grad_totals = step_grads
        else:
            grad_totals = tuple(
                (
                    first_term + second_term
                    for first_term, second_term in zip(grad_totals, step_grads)
                )
            )
    scattered = jax.tree.map(
        lambda part: part.astype(jnp.float32),
        lax.psum_scatter(as_sent(grad_totals), "fsdp", scatter_dimension=0, tiled=True),
    )
    summed = jax.tree.map(
        lambda part: part.astype(jnp.float32), lax.psum(as_sent(scattered), "ctx")
    )
    return (jnp.stack(out_list), jnp.stack(grad_list)) + tuple(summed)


def solution(mesh):
    placed = (
        P(None, "fsdp", "ctx", None),
        P(None, "fsdp"),
        P(None, "fsdp", "ctx", None),
        P("fsdp", None),
        P("fsdp"),
        P("fsdp"),
        P("fsdp", None),
        P("fsdp"),
        P("fsdp"),
        P("fsdp"),
        P("fsdp", None),
        P("fsdp"),
        P("fsdp", None),
        P("fsdp"),
        P("fsdp"),
        P("fsdp"),
    )
    return jax.shard_map(
        body,
        mesh=mesh,
        in_specs=placed,
        out_specs=(
            P(None, "fsdp", "ctx", None),
            P(None, "fsdp", "ctx", None),
            P("fsdp", None),
            P("fsdp"),
            P("fsdp"),
            P("fsdp", None),
            P("fsdp"),
            P("fsdp"),
            P("fsdp"),
            P("fsdp", None),
            P("fsdp"),
            P("fsdp", None),
            P("fsdp"),
            P("fsdp"),
            P("fsdp"),
        ),
        check_vma=False,
    )
```

profile of v0, /device:TPU:0, one launch (start us, length us, event | category | flops | bytes accessed | tf_op | source)
XLA Modules:
  0.0 1426.1 jit_solution(1560825900270771774)
XLA Ops:
  8.6 12.6 all-gather.1
  30.4 14.3 %all-gather.2 = bf16[4,1,256]{2,1,0:T(2,128)(2,1)S(1)} all-gather(bf16[1,1,256]{2,1,0:T(2,128)(2,1)S(1)} %reshape.466), channel_id=1, replica_groups=mesh['ctx'=8,'fsdp'=4] {'fsdp'}, dimensions={0}, use_global_device_ids=true | all-gather | bytes 2560 | tf_op jit(solution)/shard_map/all_gather | solution.py:93
  57.3 70.5 %all-gather.15.cloned.1.call-done = bf16[1024,3072]{1,0:T(8,128)(2,1)} async-done(((bf16[256,3072]{1,0:T(8,128)(2,1)}), bf16[1024,3072]{1,0:T(8,128)(2,1)}) %all-gather.15.cloned.1.call-update) | async-done | bytes 6291472 | tf_op jit(solution)/shard_map/all_gather | solution.py:92
  153.7 11.9 all_gather.79
  219.4 13.6 fusion.36
  233.5 13.1 all-gather.17.cloned.1.call-done
  276.1 12.4 fusion.37
  300.2 143.6 %all-gather.21.cloned.1.call-done = bf16[1024,4096]{1,0:T(8,128)(2,1)} async-done(((bf16[256,4096]{1,0:T(8,128)(2,1)}), bf16[1024,4096]{1,0:T(8,128)(2,1)}) %all-gather.21.cloned.1.call-update) | async-done | bytes 8388624 | tf_op jit(solution)/shard_map/all_gather | solution.py:99
  456.6 136.5 %all-gather.23.cloned.1.call-done = bf16[4096,1024]{1,0:T(8,128)(2,1)} async-done(((bf16[1024,1024]{1,0:T(8,128)(2,1)}), bf16[4096,1024]{1,0:T(8,128)(2,1)}) %all-gather.23.cloned.1.call-update) | async-done | bytes 8388624 | tf_op jit(solution)/shard_map/all_gather | solution.py:101
  593.1 16.8 %convert_reduce_fusion = (f32[4096]{0:T(1024)}, bf16[256,4096]{1,0:T(8,128)(2,1)S(1)}, f32[256,4096]{1,0:T(8,128)}) fusion(f32[256,4096]{1,0:T(8,128)} %convolution_add_fusion, bf16[256,1024]{1,0:T(8,128)(2,1)} %get-tuple-element.90, bf16[4096,1024]{1,0:T(8,128)(2,1)} %all-gather.23.cloned.1.call-done), kind=kOutput, calls=%fused_computation.25 | convolution fusion | flops 2225074176 | bytes 19415040 | tf_op jit(solution)/shard_map/dot_general | solution.py:44
  617.9 14.7 %convert_reduce_fusion.1 = (f32[4096]{0:T(1024)}, bf16[256,4096]{1,0:T(8,128)(2,1)S(1)}, f32[256,4096]{1,0:T(8,128)}) fusion(f32[256,4096]{1,0:T(8,128)S(1)} %copy-done.37, bf16[256,1024]{1,0:T(8,128)(2,1)S(1)} %copy-done.56, bf16[4096,1024]{1,0:T(8,128)(2,1)S(1)} %copy-done.107), kind=kOutput, calls=%fused_computation.26 | convolution fusion | flops 2225074176 | bytes 19415040 | tf_op jit(solution)/shard_map/dot_general | solution.py:44
  648.7 13.0 convolution_convert_fusion
  669.7 11.5 multiply_convert_fusion
  705.3 13.8 convolution_convert_fusion.1
  725.9 11.1 multiply_convert_fusion.1
  770.6 12.1 add_convert_fusion.1
  798.9 11.6 add_convert_fusion
  861.4 11.8 all-gather.7
  892.6 145.5 %reduce-scatter.15.cloned.1.call-done = bf16[256,4096]{1,0:T(8,128)(2,1)} async-done(((bf16[1024,4096]{1,0:T(8,128)(2,1)}), bf16[256,4096]{1,0:T(8,128)(2,1)}) %reduce-scatter.15.cloned.1.call-update) | async-done | bytes 2097168 | tf_op jit(solution)/shard_map/reduce_scatter | solution.py:304
  1038.1 147.7 %reduce-scatter.17.cloned.1.call-done = bf16[1024,1024]{1,0:T(8,128)(2,1)} async-done(((bf16[4096,1024]{1,0:T(8,128)(2,1)}), bf16[1024,1024]{1,0:T(8,128)(2,1)}) %reduce-scatter.17.cloned.1.call-update) | async-done | bytes 2097168 | tf_op jit(solution)/shard_map/reduce_scatter | solution.py:304
  1185.8 113.8 %reduce-scatter.11.cloned.1.call-done = bf16[256,3072]{1,0:T(8,128)(2,1)} async-done(((bf16[1024,3072]{1,0:T(8,128)(2,1)}), bf16[256,3072]{1,0:T(8,128)(2,1)}) %reduce-scatter.11.cloned.1.call-update) | async-done | bytes 1572880 | tf_op jit(solution)/shard_map/reduce_scatter | solution.py:304
  1308.3 18.2 %all-reduce.11 = (bf16[1024]{0:T(1024)(128)(2,1)S(1)}, bf16[1024]{0:T(1024)(128)(2,1)S(1)}, bf16[1024]{0:T(1024)(128)(2,1)S(1)}, bf16[1024]{0:T(1024)(128)(2,1)S...) all-reduce(bf16[1024]{0:T(1024)(128)(2,1)S(1)} %add_convert_fusion., ...), channel_id=5, replica_groups=mesh['ctx'=8,'fsdp'=4] {'fsdp'}, use_global_device_ids=true, to_apply=%region_28.29.clone | all-reduce | flops 12288 | bytes 49152
  1327.1 13.0 all-reduce.9
  1349.3 60.1 %all-reduce.14.cloned.1.call-done = (bf16[256,3072]{1,0:T(8,128)(2,1)}, bf16[256,1024]{1,0:T(8,128)(2,1)}, bf16[256,4096]{1,0:T(8,128)(2,1)}, bf16[1024,1024]{1,0:T(8,128)(2,1)}) async-done(((bf16[256,3072]{1,0:T(8,128)(2,1)}, bf16[256,1024]{1,0:T(8,128)(2,1)}, bf16[256,4096]{1,0:T(8,128)(2,1)}, bf16[1024,1024]{1,0:T(8,128)(2,1)}), (bf16[256,3072]{1,0:T(8,128)(2,1)}, bf16[256,1024]{1,0:T(8,128)(2,1)}, ...) | async-done | bytes 6291472 | tf_op jit(solution)/shard_map/psum | solution.py:307
  (431 shorter events, 365.6 us)
Async XLA Ops:
  7.2 120.6 %all-gather.15.cloned.1.call-start = ((), (), s32[]{:S(2)}) async-start(), calls=%async_computation.6 | async-start | bytes 7864320 | tf_op jit(solution)/shard_map/all_gather | solution.py:92
  7.9 182.3 %all-gather.25.cloned.1.call-start = ((), (), s32[]{:S(2)}) async-start(), calls=%async_computation.11 | async-start | bytes 9437184 | tf_op jit(solution)/shard_map/all_gather | solution.py:135
  54.6 77.9 %copy-start.87 = (f32[256]{0:T(256)}, f32[256]{0:T(256)S(1)}, u32[]{:S(2)}) copy-start(f32[256]{0:T(256)S(1)} %get-tuple-element.108) | copy-start | bytes 3076
  137.4 109.2 %all-gather.17.cloned.1.call-start = ((), (), s32[]{:S(2)}) async-start(), calls=%async_computation.7 | async-start | bytes 9437184 | tf_op jit(solution)/shard_map/all_gather | solution.py:135
  139.9 154.1 %all-gather.19.cloned.1.call-start = ((), (), s32[]{:S(2)}) async-start(), calls=%async_computation.8 | async-start | bytes 2621440 | tf_op jit(solution)/shard_map/all_gather | solution.py:95
  140.5 303.3 %all-gather.21.cloned.1.call-start = ((), (), s32[]{:S(2)}) async-start(), calls=%async_computation.9 | async-start | bytes 10485760 | tf_op jit(solution)/shard_map/all_gather | solution.py:99
  141.2 452.0 %all-gather.23.cloned.1.call-start = ((), (), s32[]{:S(2)}) async-start(), calls=%async_computation.10 | async-start | bytes 10485760 | tf_op jit(solution)/shard_map/all_gather | solution.py:101
  141.7 687.4 %reduce-scatter.9.cloned.1.call-start = ((), (), s32[]{:S(2)}) async-start(), calls=%async_computation.13 | async-start | bytes 9437184 | tf_op jit(solution)/shard_map/reduce_scatter | solution.py:263
  145.7 130.4 %copy-start.45 = (pred[2,128,1024]{2,1,0:T(8,128)(4,1)}, pred[2,128,1024]{2,1,0:T(8,128)(4,1)S(1)}, u32[]{:S(2)}) copy-start(pred[2,128,1024]{2,1,0:T(8,128)(4,1)S(1)} %get-tuple-element.93) | copy-start | bytes 786436
  173.9 278.2 %copy-start.65 = (f32[4,1,256]{2,1,0:T(1,128)}, f32[4,1,256]{2,1,0:T(1,128)S(1)}, u32[]{:S(2)}) copy-start(f32[4,1,256]{2,1,0:T(1,128)S(1)} %convert_element_type.423) | copy-start | bytes 12292
  187.1 78.4 %copy-start.21 = (bf16[2,128,16,64]{1,3,2,0:T(8,128)(2,1)}, bf16[2,128,16,64]{1,3,2,0:T(8,128)(2,1)S(1)}, u32[]{:S(2)}) copy-start(bf16[2,128,16,64]{1,3,2,0:T(8,128)(2,1)S(1)} %copy.67) | copy-start | bytes 1572868
  700.4 144.8 %reduce-scatter.7.cloned.1.call-start = ((), (), s32[]{:S(2)}) async-start(), calls=%async_computation.12 | async-start | bytes 9437184 | tf_op jit(solution)/shard_map/reduce_scatter | solution.py:263
  756.3 136.3 %reduce-scatter.13.cloned.1.call-start = ((), (), s32[]{:S(2)}) async-start(), calls=%async_computation.15 | async-start | bytes 2621440 | tf_op jit(solution)/shard_map/reduce_scatter | solution.py:304
  760.3 277.8 %reduce-scatter.15.cloned.1.call-start = ((), (), s32[]{:S(2)}) async-start(), calls=%async_computation.16 | async-start | bytes 10485760 | tf_op jit(solution)/shard_map/reduce_scatter | solution.py:304
  782.8 403.0 %reduce-scatter.17.cloned.1.call-start = ((), (), s32[]{:S(2)}) async-start(), calls=%async_computation.17 | async-start | bytes 10485760 | tf_op jit(solution)/shard_map/reduce_scatter | solution.py:304
  810.5 489.1 %reduce-scatter.11.cloned.1.call-start = ((), (), s32[]{:S(2)}) async-start(), calls=%async_computation.14 | async-start | bytes 7864320 | tf_op jit(solution)/shard_map/reduce_scatter | solution.py:304
  860.8 548.6 %all-reduce.14.cloned.1.call-start = ((), (), s32[]{:S(2)}) async-start(), calls=%async_computation.18 | async-start | bytes 12582912 | tf_op jit(solution)/shard_map/psum | solution.py:307
  892.5 407.1 %copy-start.39 = (f32[256,1024]{1,0:T(8,128)}, f32[256,1024]{1,0:T(8,128)S(1)}, u32[]{:S(2)}) copy-start(f32[256,1024]{1,0:T(8,128)S(1)} %fusion.40) | copy-start | bytes 3145732
  892.5 407.1 %copy-start.4 = (bf16[2,2,128,1024]{3,2,1,0:T(8,128)(2,1)S(1)}, bf16[2,2,128,1024]{3,2,1,0:T(8,128)(2,1)}, u32[]{:S(2)}) copy-start(bf16[2,2,128,1024]{3,2,1,0:T(8,128)(2,1)} %param.16) | copy-start | bytes 3145732
  892.5 407.1 %copy-start.58 = (bf16[128,8,2,128]{3,1,2,0:T(8,128)(2,1)S(1)}, bf16[128,8,2,128]{3,1,2,0:T(8,128)(2,1)}, u32[]{:S(2)}) copy-start(bf16[128,8,2,128]{3,1,2,0:T(8,128)(2,1)} %copy.136) | copy-start | bytes 1572868
  892.5 407.1 %copy-start.59 = (bf16[256,1024]{0,1:T(8,128)(2,1)S(1)}, bf16[256,1024]{0,1:T(8,128)(2,1)}, u32[]{:S(2)}) copy-start(bf16[256,1024]{0,1:T(8,128)(2,1)} %copy.82) | copy-start | bytes 1572868
  892.5 407.1 %copy-start.70 = (f32[4,1,256]{2,1,0:T(1,128)S(1)}, f32[4,1,256]{2,1,0:T(1,128)}, u32[]{:S(2)}) copy-start(f32[4,1,256]{2,1,0:T(1,128)} %copy-done.69) | copy-start | bytes 12292
  892.5 407.1 %copy-start.88 = (f32[256]{0:T(256)S(1)}, f32[256]{0:T(256)}, u32[]{:S(2)}) copy-start(f32[256]{0:T(256)} %copy-done.87) | copy-start | bytes 3076
  892.5 407.1 %copy-start.90 = (f32[256]{0:T(256)S(1)}, f32[256]{0:T(256)}, u32[]{:S(2)}) copy-start(f32[256]{0:T(256)} %copy-done.89) | copy-start | bytes 3076
  (106 other events, 1445.4 us)
Sparse Core Ops, SparseCore 0:
  9.6 118.1 all-gather.14
  137.6 52.6 all-gather.24
  192.2 54.3 all-gather.16
  248.0 45.9 all-gather.18
  295.4 148.3 all-gather.20
  445.2 147.8 all-gather.22
  700.5 69.4 reduce-scatter.8
  773.9 71.2 reduce-scatter.6
  848.0 43.8 reduce-scatter.12
  894.3 143.7 reduce-scatter.14
  1040.6 145.1 reduce-scatter.16
  1188.1 111.4 reduce-scatter.10
  1303.6 105.7 all-reduce.13
where the time goes:
time: 1430 us
  waiting for transfers between devices  850 us (59%)
  matrix products  256 us (18%)
  blocking collectives  123 us (9%)
  local copies, waits for them, and re-layouts  105 us (7%)
  other arithmetic  74.4 us (5%)
  between operations  17.4 us (1%)
    reduce_scatter x4, waiting for transfers between devices, body(): lax.psum_scatter(as_sent(grad_totals), 'fsdp', scatter_dimension=0, tiled...  407 us
    dot_general x24, matrix products, matmul(): return jnp.dot(left_side, right_side, preferred_element_type=jnp.float32)  149 us
    all_gather x1, waiting for transfers between devices, body(): lax.all_gather(shards[7], 'fsdp', axis=0, tiled=True)  144 us
    all_gather x1, waiting for transfers between devices, body(): lax.all_gather(shards[9], 'fsdp', axis=0, tiled=True)  137 us
    all_gather x1, waiting for transfers between devices, body(): lax.all_gather(shards[0], 'fsdp', axis=0, tiled=True)  70.5 us
    psum x1, waiting for transfers between devices, body(): lax.psum(as_sent(scattered), 'ctx')  60.1 us
  transfers between devices with their start and end apart: 13, of which 11 were waited for; matrix products, arithmetic and copies ran while one was open for 21% of the time, Pallas kernels for 0%

commit v1 on v0

v1 whole, which is shorter than its diff:
```python
import functools

import jax
import jax.numpy as jnp
from jax import lax
from jax.experimental import pallas as pl
from jax.experimental.pallas import tpu as pltpu
from jax.sharding import PartitionSpec as P

HEADS = 16
HEAD_DIM = 64
EPS = 1e-05
NEG_FILL = -1e30
MESH = pl.DeviceIdType.MESH
F32 = jnp.float32
BF16 = jnp.bfloat16
VMEM = pltpu.VMEM
DMA = pltpu.SemaphoreType.DMA
VMEM_LIMIT = 60 * 1024 * 1024
CHUNKS = 12


def layer_norm(inputs, ln_gain, ln_shift):
    center = jnp.mean(inputs, axis=-1, keepdims=True)
    centered = inputs - center
    spread = jnp.mean(centered * centered, axis=-1, keepdims=True)
    return centered * lax.rsqrt(spread + EPS) * ln_gain + ln_shift


def rows_sum(matrix):
    return jnp.sum(matrix.astype(F32), axis=0)


def matmul(left_side, right_side):
    return jnp.dot(left_side, right_side, preferred_element_type=F32)


def dot_nt(a, b):
    return lax.dot_general(a, b, (((1,), (1,)), ((), ())), preferred_element_type=F32)


def dot_tn(a, b):
    return lax.dot_general(a, b, (((0,), (0,)), ((), ())), preferred_element_type=F32)


def place():
    d = lax.axis_index("ctx")
    z = lax.axis_index("fsdp")
    return d, d // 4, lax.rem(d // 2, 2), lax.rem(d, 2), z


def remote(src, dst, send, recv, device):
    return pltpu.make_async_remote_copy(
        src_ref=src, dst_ref=dst, send_sem=send, recv_sem=recv, device_id=device, device_id_type=MESH
    )


def greet(devices):
    barrier = pltpu.get_barrier_semaphore()
    for device in devices:
        pl.semaphore_signal(barrier, inc=1, device_id=device, device_id_type=MESH)
    pl.semaphore_wait(barrier, len(devices))


def run_stages(stages, offsets, count):
    @pl.loop(0, count + offsets[-1])
    def _(step):
        for index in reversed(range(len(stages))):
            chunk = step - offsets[index]

            @pl.when((chunk >= 0) & (chunk < count))
            def _():
                stages[index](chunk)


def gather_kernel(count, offsets, src, small, out, small_out, local_sem, vs, vr, zs, zr, xs, xr, cs, cr):
    d, y, x, c, z = place()
    x_nb, y_nb, c_nb = (d + 2 - 4 * x, z), (d + 4 - 8 * y, z), (d + 1 - 2 * c, z)
    line = [(d, lax.rem(z + k, 4)) for k in (1, 2, 3)]
    greet([x_nb, y_nb, c_nb] + line)
    local = pltpu.make_async_copy(src, out.at[:, z], local_sem)
    local.start()

    def small_copy(k):
        return remote(small, small_out.at[z], vs.at[k], vr.at[k], line[k])

    def small_recv(k):
        return remote(small, small_out.at[lax.rem(z + 3 - k, 4)], vs.at[k], vr.at[k], line[k])

    for k in range(3):
        small_copy(k).start()
    small_out[z] = small[...]

    def z_copy(chunk, k, down):
        piece = z + k if down else z - k
        ref = src.at[chunk, y, x, c] if k == 0 else out.at[chunk, piece, y, x, c]
        target = (d, z - 1) if down else (d, z + 1)
        return remote(ref, out.at[chunk, piece, y, x, c], zs.at[chunk, down, k], zr.at[chunk, down, k], target)

    def z_recv(chunk, k, down):
        piece = z + 1 + k if down else z - 1 - k
        ref = out.at[chunk, piece, y, x, c]
        return remote(ref, ref, zs.at[chunk, down, k], zr.at[chunk, down, k], x_nb)

    def z_start(chunk, k):
        @pl.when((z < 3) & (z >= k))
        def _():
            z_copy(chunk, k, 0).start()

        @pl.when((z > 0) & (z + k <= 3))
        def _():
            z_copy(chunk, k, 1).start()

    def z_wait(chunk, k):
        @pl.when(z >= k + 1)
        def _():
            z_recv(chunk, k, 0).wait_recv()

        @pl.when(z + k + 1 <= 3)
        def _():
            z_recv(chunk, k, 1).wait_recv()

    def first(chunk, i, axis):
        ref = out.at[chunk, lax.rem(z + 1 + i, 4), y, x, c, axis]
        return remote(ref, ref, xs.at[chunk, 0, axis, i], xr.at[chunk, 0, axis, i], y_nb if axis else x_nb)

    def first_recv(chunk, i, axis):
        piece = lax.rem(z + 1 + i, 4)
        ref = out.at[chunk, piece, 1 - y, x, c, 1] if axis else out.at[chunk, piece, y, 1 - x, c, 0]
        return remote(ref, ref, xs.at[chunk, 0, axis, i], xr.at[chunk, 0, axis, i], y_nb if axis else x_nb)

    def second(chunk, i, axis):
        piece = lax.rem(z + 1 + i, 4)
        ref = out.at[chunk, piece, :, x, c, 1] if axis else out.at[chunk, piece, y, :, c, 0]
        return remote(ref, ref, xs.at[chunk, 1, axis, i], xr.at[chunk, 1, axis, i], x_nb if axis else y_nb)

    def second_recv(chunk, i, axis):
        piece = lax.rem(z + 1 + i, 4)
        ref = out.at[chunk, piece, :, 1 - x, c, 1] if axis else out.at[chunk, piece, 1 - y, :, c, 0]
        return remote(ref, ref, xs.at[chunk, 1, axis, i], xr.at[chunk, 1, axis, i], x_nb if axis else y_nb)

    def across(chunk, i, core):
        ref = out.at[chunk, lax.rem(z + 1 + i, 4), :, :, core]
        return remote(ref, ref, cs.at[chunk, i], cr.at[chunk, i], c_nb)

    def stage0(chunk):
        z_start(chunk, 0)

    def stage1(chunk):
        z_wait(chunk, 0)
        z_start(chunk, 1)

    def stage2(chunk):
        z_wait(chunk, 1)
        z_start(chunk, 2)

    def stage3(chunk):
        z_wait(chunk, 2)
        for i in range(3):
            for axis in range(2):
                first(chunk, i, axis).start()

    def stage4(chunk):
        for i in range(3):
            for axis in range(2):
                first_recv(chunk, i, axis).wait_recv()
        for i in range(3):
            for axis in range(2):
                second(chunk, i, axis).start()

    def stage5(chunk):
        for i in range(3):
            for axis in range(2):
                second_recv(chunk, i, axis).wait_recv()
        for i in range(3):
            across(chunk, i, c).start()

    def stage6(chunk):
        for i in range(3):
            across(chunk, i, 1 - c).wait_recv()
        for i in range(3):
            across(chunk, i, c).wait_send()
            for axis in range(2):
                first(chunk, i, axis).wait_send()
                second(chunk, i, axis).wait_send()
        for k in range(3):
            @pl.when((z < 3) & (z >= k))
            def _():
                z_copy(chunk, k, 0).wait_send()

            @pl.when((z > 0) & (z + k <= 3))
            def _():
                z_copy(chunk, k, 1).wait_send()

    run_stages([stage0, stage1, stage2, stage3, stage4, stage5, stage6], offsets, count)
    for k in range(3):
        small_recv(k).wait_recv()
        small_copy(k).wait_send()
    local.wait()


def gather_weights(packed, small):
    count, rows, width = packed.shape
    vm, anywhere = pl.BlockSpec(memory_space=VMEM), pl.BlockSpec(memory_space=pl.ANY)
    out, small_out = pl.pallas_call(
        functools.partial(gather_kernel, count, (0, 1, 2, 3, 5, 7, 8)),
        out_shape=(
            jax.ShapeDtypeStruct((count, 4, 2, 2, 2, 2, rows // 16, width), BF16),
            jax.ShapeDtypeStruct((4,) + small.shape, BF16),
        ),
        in_specs=[vm, vm],
        out_specs=(anywhere, vm),
        scratch_shapes=[
            DMA, DMA((3,)), DMA((3,)),
            DMA((count, 2, 3)), DMA((count, 2, 3)),
            DMA((count, 2, 2, 3)), DMA((count, 2, 2, 3)),
            DMA((count, 3)), DMA((count, 3)),
        ],
        compiler_params=pltpu.CompilerParams(
            collective_id=0, has_side_effects=True, vmem_limit_bytes=24 * 1024 * 1024
        ),
        name="gather_weights",
    )(packed.reshape(count, 2, 2, 2, 2, rows // 16, width), small)
    return out.reshape(count, 4 * rows, width), small_out


def reduce_kernel(
    bounds, offsets, *refs
):
    count = bounds[-1]
    parts, small = refs[: len(bounds) - 1], refs[len(bounds) - 1]
    out, small_out = refs[len(bounds)], refs[len(bounds) + 1]
    (acc, core_in, x_in, y_in, x_in2, y_in2, up_in, down_in, small_in,
     ls, cs, cr, s1, r1, s2, r2, zs, zr, s3, r3, s4, r4, s5, r5, vs, vr) = refs[len(bounds) + 2 :]
    d, y, x, c, z = place()
    x_nb, y_nb, c_nb = (d + 2 - 4 * x, z), (d + 4 - 8 * y, z), (d + 1 - 2 * c, z)
    line = [(d, lax.rem(z + k, 4)) for k in (1, 2, 3)]
    greet([x_nb, y_nb, c_nb] + line)

    def load(ref, chunk, slot):
        return pltpu.make_async_copy(ref.at[chunk, :, :, :, c], acc.at[slot], ls.at[slot])

    def core_send(ref, chunk, slot):
        return remote(ref.at[chunk, :, :, :, 1 - c], core_in.at[slot], cs.at[slot], cr.at[slot], c_nb)

    def x1(k):
        return remote(acc.at[k, :, :, 1 - x, 0], x_in.at[k], s1.at[k, 0], r1.at[k, 0], x_nb)

    def y1(k):
        return remote(acc.at[k, :, 1 - y, :, 1], y_in.at[k], s1.at[k, 1], r1.at[k, 1], y_nb)

    def y2(k):
        return remote(acc.at[k, :, 1 - y, x, 0], y_in2.at[k], s2.at[k, 0], r2.at[k, 0], y_nb)

    def x2(k):
        return remote(acc.at[k, :, y, 1 - x, 1], x_in2.at[k], s2.at[k, 1], r2.at[k, 1], x_nb)

    def up(k, i):
        return remote(acc.at[k, z + 3 - i, y, x], up_in.at[k, i], zs.at[k, 0, i], zr.at[k, 0, i], (d, z + 1))

    def down(k, i):
        return remote(acc.at[k, z - 3 + i, y, x], down_in.at[k, i], zs.at[k, 1, i], zr.at[k, 1, i], (d, z - 1))

    def up_wait(k, i):
        remote(up_in.at[k, i], up_in.at[k, i], zs.at[k, 0, i], zr.at[k, 0, i], c_nb).wait_recv()

    def down_wait(k, i):
        remote(down_in.at[k, i], down_in.at[k, i], zs.at[k, 1, i], zr.at[k, 1, i], c_nb).wait_recv()

    def g1(k, axis):
        ref = out.at[k, y, x, c, axis]
        return remote(ref, ref, s3.at[k, axis], r3.at[k, axis], y_nb if axis else x_nb)

    def g1_recv(k, axis):
        ref = out.at[k, 1 - y, x, c, 1] if axis else out.at[k, y, 1 - x, c, 0]
        return remote(ref, ref, s3.at[k, axis], r3.at[k, axis], y_nb if axis else x_nb)

    def g2(k, axis):
        ref = out.at[k, :, x, c, 1] if axis else out.at[k, y, :, c, 0]
        return remote(ref, ref, s4.at[k, axis], r4.at[k, axis], x_nb if axis else y_nb)

    def g2_recv(k, axis):
        ref = out.at[k, :, 1 - x, c, 1] if axis else out.at[k, 1 - y, :, c, 0]
        return remote(ref, ref, s4.at[k, axis], r4.at[k, axis], x_nb if axis else y_nb)

    def g3(k, core):
        ref = out.at[k, :, :, core]
        return remote(ref, ref, s5.at[k], r5.at[k], c_nb)

    def z_send(k, i):
        @pl.when((z < 3) & (z <= i))
        def _():
            up(k, i).start()

        @pl.when((z > 0) & (z >= 3 - i))
        def _():
            down(k, i).start()

    def z_add(k, i):
        @pl.when((z >= 1) & (z - 1 <= i))
        def _():
            up_wait(k, i)
            acc[k, z + 2 - i, y, x] += up_in[k, i]

        @pl.when((z <= 2) & (z + 1 >= 3 - i))
        def _():
            down_wait(k, i)
            acc[k, z - 2 + i, y, x] += down_in[k, i]

    def stage0(k):
        for index, part in enumerate(parts):
            low, high = bounds[index], bounds[index + 1]

            @pl.when((k >= low) & (k < high))
            def _():
                core_send(part, k - low, k).start()
                load(part, k - low, k).start()

    def stage1(k):
        load(parts[0], 0, k).wait()
        core_send(parts[0], 0, k).wait_recv()
        for piece in range(4):
            acc[k, piece] += core_in[k, piece]
        x1(k).start()
        y1(k).start()

    def stage2(k):
        x1(k).wait_recv()
        y1(k).wait_recv()
        acc[k, :, :, x, 0] += x_in[k]
        acc[k, :, y, :, 1] += y_in[k]
        y2(k).start()
        x2(k).start()

    def stage3(k):
        y2(k).wait_recv()
        x2(k).wait_recv()
        acc[k, :, y, x, 0] += y_in2[k]
        acc[k, :, y, x, 1] += x_in2[k]
        z_send(k, 0)

    def stage4(k):
        z_add(k, 0)
        z_send(k, 1)

    def stage5(k):
        z_add(k, 1)
        z_send(k, 2)

    def stage6(k):
        z_add(k, 2)
        out[k, y, x, c] = acc[k, z, y, x]
        g1(k, 0).start()
        g1(k, 1).start()

    def stage7(k):
        for axis in range(2):
            g1_recv(k, axis).wait_recv()
        for axis in range(2):
            g2(k, axis).start()

    def stage8(k):
        for axis in range(2):
            g2_recv(k, axis).wait_recv()
        g3(k, c).start()

    def stage9(k):
        g3(k, 1 - c).wait_recv()
        g3(k, c).wait_send()
        core_send(parts[0], 0, k).wait_send()
        x1(k).wait_send()
        y1(k).wait_send()
        x2(k).wait_send()
        y2(k).wait_send()
        for axis in range(2):
            g1(k, axis).wait_send()
            g2(k, axis).wait_send()
        for i in range(3):
            @pl.when((z < 3) & (z <= i))
            def _():
                up(k, i).wait_send()

            @pl.when((z > 0) & (z >= 3 - i))
            def _():
                down(k, i).wait_send()

    for step, nb in enumerate((c_nb, x_nb, y_nb)):
        if step == 0:
            small_out[0] = small[...]
        copy = remote(small_out.at[step], small_in.at[step], vs.at[step], vr.at[step], nb)
        copy.start()
        copy.wait()
        small_out[step + 1] = small_out[step] + small_in[step]
    copies = [remote(small_out.at[3], small_in.at[3 + k], vs.at[3 + k], vr.at[3 + k], line[k]) for k in range(3)]
    for copy in copies:
        copy.start()

    run_stages(
        [stage0, stage1, stage2, stage3, stage4, stage5, stage6, stage7, stage8, stage9], offsets, count
    )
    for copy in copies:
        copy.wait()
    small_out[4] = small_out[3] + small_in[3] + small_in[4] + small_in[5]


def reduce_gradients(parts, small, collective):
    rows, width = parts[0].shape[1] // 4, parts[0].shape[2]
    piece = rows // 16
    bounds = [0]
    for part in parts:
        bounds.append(bounds[-1] + part.shape[0])
    n = bounds[-1]
    vm, anywhere = pl.BlockSpec(memory_space=VMEM), pl.BlockSpec(memory_space=pl.ANY)
    out, small_out = pl.pallas_call(
        functools.partial(reduce_kernel, tuple(bounds), (0, 1, 3, 5, 6, 7, 8, 9, 10, 11)),
        out_shape=(
            jax.ShapeDtypeStruct((n, 2, 2, 2, 2, piece, width), BF16),
            jax.ShapeDtypeStruct((5,) + small.shape, F32),
        ),
        in_specs=[anywhere] * len(parts) + [vm],
        out_specs=(vm, vm),
        scratch_shapes=[
            VMEM((n, 4, 2, 2, 2, piece, width), BF16),
            VMEM((n, 4, 2, 2, 2, piece, width), BF16),
            VMEM((n, 4, 2, piece, width), BF16),
            VMEM((n, 4, 2, piece, width), BF16),
            VMEM((n, 4, piece, width), BF16),
            VMEM((n, 4, piece, width), BF16),
            VMEM((n, 3, 2, piece, width), BF16),
            VMEM((n, 3, 2, piece, width), BF16),
            VMEM((6,) + small.shape, F32),
            DMA((n,)), DMA((n,)), DMA((n,)),
            DMA((n, 2)), DMA((n, 2)), DMA((n, 2)), DMA((n, 2)),
            DMA((n, 2, 3)), DMA((n, 2, 3)),
            DMA((n, 2)), DMA((n, 2)), DMA((n, 2)), DMA((n, 2)),
            DMA((n,)), DMA((n,)), DMA((6,)), DMA((6,)),
        ],
        compiler_params=pltpu.CompilerParams(
            collective_id=collective, has_side_effects=True, vmem_limit_bytes=VMEM_LIMIT
        ),
        name="reduce_gradients",
    )(*[p.reshape(p.shape[0], 4, 2, 2, 2, 2, piece, width) for p in parts], small)
    return out.reshape(n, rows, width), small_out[4]


def head_lanes(width):
    return lax.broadcasted_iota(jnp.int32, (1, width), 1) // HEAD_DIM


def attend(q, k, v, length, block, put):
    slots = k.shape[0]
    key_pos = lax.broadcasted_iota(jnp.int32, (1, slots), 1)
    bias = jnp.where(key_pos < length, 0.0, NEG_FILL).astype(F32)
    width = k.shape[1]
    lanes = head_lanes(width)
    causal = lax.broadcasted_iota(jnp.int32, (block, block), 1) <= lax.broadcasted_iota(
        jnp.int32, (block, block), 0
    )
    for start in range(0, slots, block):
        stop = start + block
        q_block = q[start:stop, :]
        sums, levels = None, None
        for head in range(width // HEAD_DIM):
            q_head = jnp.where(lanes == head, q_block, jnp.zeros_like(q_block)) * jnp.asarray(HEAD_DIM**-0.5, BF16)
            scores = dot_nt(q_head, k[:stop, :]) + bias[:, :stop]
            last = jnp.where(causal, scores[:, start:], NEG_FILL)
            top = jnp.max(last, axis=1, keepdims=True)
            if start:
                top = jnp.maximum(top, jnp.max(scores[:, :start], axis=1, keepdims=True))
                scores = jnp.concatenate([scores[:, :start], last], axis=1)
            else:
                scores = last
            weights = jnp.exp(scores - top)
            total = jnp.sum(weights, axis=1, keepdims=True)
            mixed = matmul(weights.astype(BF16), v[:stop, :]) / total
            level = top + jnp.log(total)
            sums = mixed if sums is None else jnp.where(lanes == head, mixed, sums)
            level = jnp.broadcast_to(level, mixed.shape)
            levels = level if levels is None else jnp.where(lanes == head, level, levels)
        put(start, stop, sums, levels)


def peers():
    d, z = lax.axis_index("ctx"), lax.axis_index("fsdp")
    to = [lax.rem(d + k, 8) for k in range(1, 8)]
    come = [lax.rem(d + 8 - k, 8) for k in range(1, 8)]
    return d, z, to, come


def lanes_of(index):
    return pl.ds(pl.multiple_of(index * 128, 128), 128)


def rows_of(index):
    return pl.ds(pl.multiple_of(index * 128, 128), 128)


def attention_forward_kernel(qkv, lengths, low_out, buf, o_out, level_out, mine, ls, s1, r1, lt, s2, r2):
    d, z, to, come = peers()
    greet([(p, z) for p in to])
    seqs = qkv.shape[1]

    def send(s, k):
        return remote(
            qkv.at[:, s, :, lanes_of(to[k])], buf.at[s, :, rows_of(d), :], s1.at[s, k], r1.at[s, k], (to[k], z)
        )

    def recv(s, k):
        ref = buf.at[s, :, rows_of(come[k]), :]
        return remote(ref, ref, s1.at[s, k], r1.at[s, k], (to[k], z))

    def keep(s):
        return pltpu.make_async_copy(qkv.at[:, s, :, lanes_of(d)], buf.at[s, :, rows_of(d), :], ls.at[s])

    def send_back(s, k):
        return remote(
            mine.at[s, rows_of(to[k]), :], low_out.at[s, :, lanes_of(d)], s2.at[s, k], r2.at[s, k], (to[k], z)
        )

    def recv_back(s, k):
        ref = low_out.at[s, :, lanes_of(come[k])]
        return remote(ref, ref, s2.at[s, k], r2.at[s, k], (to[k], z))

    def keep_back(s):
        return pltpu.make_async_copy(mine.at[s, rows_of(d), :], low_out.at[s, :, lanes_of(d)], lt.at[s])

    @pl.loop(0, seqs)
    def _(s):
        for k in range(7):
            send(s, k).start()
        keep(s).start()

    @pl.loop(0, seqs)
    def _(s):
        keep(s).wait()
        for k in range(7):
            recv(s, k).wait_recv()

        def put(start, stop, mixed, level):
            o_out[s, start:stop, :] = mixed
            level_out[s, start:stop, :] = level
            mine[s, start:stop, :] = mixed.astype(BF16)

        attend(buf.at[s, 0], buf.at[s, 1], buf.at[s, 2], lengths[s], 256, put)
        for k in range(7):
            send_back(s, k).start()
        keep_back(s).start()

    @pl.loop(0, seqs)
    def _(s):
        keep_back(s).wait()
        for k in range(7):
            recv_back(s, k).wait_recv()
            send(s, k).wait_send()
            send_back(s, k).wait_send()


def attention_forward(qkv, lengths):
    _, seqs, slots, width = qkv.shape
    vm = pl.BlockSpec(memory_space=VMEM)
    return pl.pallas_call(
        attention_forward_kernel,
        out_shape=(
            jax.ShapeDtypeStruct((seqs, slots, width), BF16),
            jax.ShapeDtypeStruct((seqs, 3, slots * 8, 128), BF16),
            jax.ShapeDtypeStruct((seqs, slots * 8, 128), F32),
            jax.ShapeDtypeStruct((seqs, slots * 8, 128), F32),
        ),
        in_specs=[vm, pl.BlockSpec(memory_space=pltpu.SMEM)],
        out_specs=(vm, vm, vm, vm),
        scratch_shapes=[
            VMEM((seqs, slots * 8, 128), BF16),
            DMA((seqs,)), DMA((seqs, 7)), DMA((seqs, 7)),
            DMA((seqs,)), DMA((seqs, 7)), DMA((seqs, 7)),
        ],
        compiler_params=pltpu.CompilerParams(
            collective_id=1, has_side_effects=True, vmem_limit_bytes=VMEM_LIMIT
        ),
        name="attention_forward",
    )(qkv, lengths)


def attend_back(q, k, v, o, levels, dm, length, block, put_query, put_key):
    slots, width = k.shape
    key_pos = lax.broadcasted_iota(jnp.int32, (1, slots), 1)
    bias = jnp.where(key_pos < length, 0.0, NEG_FILL).astype(F32)
    lanes = head_lanes(width)
    causal = lax.broadcasted_iota(jnp.int32, (block, block), 1) <= lax.broadcasted_iota(
        jnp.int32, (block, block), 0
    )
    scale = jnp.asarray(HEAD_DIM**-0.5, BF16)
    for start in range(0, slots, block):
        stop = start + block
        q_block = q[start:stop, :] * scale
        d_block = dm[start:stop, :]
        product = d_block.astype(F32) * o[start:stop, :]
        q_turned, d_turned = q_block.T, d_block.T
        d_query, d_keys, d_values = None, [], []
        for head in range(width // HEAD_DIM):
            here = lanes == head
            q_head = jnp.where(here, q_block, jnp.zeros_like(q_block))
            d_head = jnp.where(here, d_block, jnp.zeros_like(d_block))
            total = jnp.sum(jnp.where(here, product, 0.0), axis=1, keepdims=True)
            level = levels[start:stop, head * HEAD_DIM : head * HEAD_DIM + 1]
            scores = dot_nt(q_head, k[:stop, :]) + bias[:, :stop]
            last = jnp.where(causal, scores[:, start:], NEG_FILL)
            scores = jnp.concatenate([scores[:, :start], last], axis=1) if start else last
            weights = jnp.exp(scores - level)
            d_weight = dot_nt(d_head, v[:stop, :]) - total
            d_score = (weights * d_weight).astype(BF16)
            part = matmul(d_score, k[:stop, :])
            d_query = part if d_query is None else jnp.where(here, part, d_query)
            cut = slice(head * HEAD_DIM, (head + 1) * HEAD_DIM)
            d_values.append(matmul(d_turned[cut, :], weights.astype(BF16)))
            d_keys.append(matmul(q_turned[cut, :], d_score))
        put_query(start, stop, d_query * (HEAD_DIM**-0.5))
        put_key(start, stop, jnp.concatenate(d_keys, axis=0), jnp.concatenate(d_values, axis=0))


def attention_backward_kernel(
    dm_home, buf, o, levels, lengths, out, dm, mine, turned, ls, s1, r1, lt, s2, r2
):
    d, z, to, come = peers()
    greet([(p, z) for p in to])
    seqs = dm_home.shape[0]

    def send(s, k):
        return remote(
            dm_home.at[s, :, lanes_of(to[k])], dm.at[s, rows_of(d), :], s1.at[s, k], r1.at[s, k], (to[k], z)
        )

    def recv(s, k):
        ref = dm.at[s, rows_of(come[k]), :]
        return remote(ref, ref, s1.at[s, k], r1.at[s, k], (to[k], z))

    def keep(s):
        return pltpu.make_async_copy(dm_home.at[s, :, lanes_of(d)], dm.at[s, rows_of(d), :], ls.at[s])

    def send_back(s, k):
        return remote(
            mine.at[s, :, rows_of(to[k]), :], out.at[:, s, :, lanes_of(d)], s2.at[s, k], r2.at[s, k], (to[k], z)
        )

    def recv_back(s, k):
        ref = out.at[:, s, :, lanes_of(come[k])]
        return remote(ref, ref, s2.at[s, k], r2.at[s, k], (to[k], z))

    def keep_back(s):
        return pltpu.make_async_copy(mine.at[s, :, rows_of(d), :], out.at[:, s, :, lanes_of(d)], lt.at[s])

    @pl.loop(0, seqs)
    def _(s):
        for k in range(7):
            send(s, k).start()
        keep(s).start()

    @pl.loop(0, seqs)
    def _(s):
        keep(s).wait()
        for k in range(7):
            recv(s, k).wait_recv()
        turned[...] = jnp.zeros_like(turned)

        def put_query(start, stop, value):
            mine[s, 0, start:stop, :] = value.astype(BF16)

        def put_key(start, stop, d_key, d_value):
            turned[0, :, :stop] += d_key
            turned[1, :, :stop] += d_value

        attend_back(
            buf.at[s, 0], buf.at[s, 1], buf.at[s, 2], o.at[s], levels.at[s], dm.at[s], lengths[s], 256,
            put_query, put_key,
        )
        mine[s, 1] = turned[0].T.astype(BF16)
        mine[s, 2] = turned[1].T.astype(BF16)
        for k in range(7):
            send_back(s, k).start()
        keep_back(s).start()

    @pl.loop(0, seqs)
    def _(s):
        keep_back(s).wait()
        for k in range(7):
            recv_back(s, k).wait_recv()
            send(s, k).wait_send()
            send_back(s, k).wait_send()


def attention_backward(dm_home, buf, o, levels, lengths):
    seqs, slots, width = dm_home.shape
    vm = pl.BlockSpec(memory_space=VMEM)
    return pl.pallas_call(
        attention_backward_kernel,
        out_shape=jax.ShapeDtypeStruct((3, seqs, slots, width), BF16),
        in_specs=[vm, vm, vm, vm, pl.BlockSpec(memory_space=pltpu.SMEM)],
        out_specs=vm,
        scratch_shapes=[
            VMEM((seqs, slots * 8, 128), BF16),
            VMEM((seqs, 3, slots * 8, 128), BF16),
            VMEM((2, 128, slots * 8), F32),
            DMA((seqs,)), DMA((seqs, 7)), DMA((seqs, 7)),
            DMA((seqs,)), DMA((seqs, 7)), DMA((seqs, 7)),
        ],
        compiler_params=pltpu.CompilerParams(
            collective_id=2, has_side_effects=True, vmem_limit_bytes=VMEM_LIMIT
        ),
        name="attention_backward",
    )(dm_home, buf, o, levels, lengths)


def feed_kernel(x, d_out, w_up, w_down, bias, y, dx, g_up, g_down, g_bias, x_turned, act, d_pre):
    tile = 256
    hidden = w_up.shape[2]

    @pl.when(pl.program_id(0) == 0)
    def _():
        y[...] = jnp.zeros_like(y)
        dx[...] = jnp.zeros_like(dx)
        x_turned[...] = x[...].T

    @pl.loop(0, hidden // tile)
    def _(n):
        cut = pl.ds(pl.multiple_of(n * tile, tile), tile)
        pre = matmul(x[...], w_up[0, :, cut]) + bias[0, :, cut].astype(F32)
        cumulative = 0.5 + 0.5 * lax.erf(pre * (0.5**0.5))
        active = (pre * cumulative).astype(BF16)
        act[:, cut] = active
        slope = cumulative + pre * (jnp.exp(-0.5 * pre * pre) * 0.3989422804014327)
        back = dot_nt(d_out[...], w_down[0, cut, :]) * slope
        low = back.astype(BF16)
        d_pre[:, cut] = low
        g_bias[0, :, cut] = jnp.sum(low.astype(F32), axis=0, keepdims=True)
        g_down[0, cut, :] = matmul(active.T, d_out[...]).astype(BF16)
        g_up[0, :, cut] = matmul(x_turned[...], low).astype(BF16)

    @pl.loop(0, y.shape[1] // tile)
    def _(n):
        cut = pl.ds(pl.multiple_of(n * tile, tile), tile)
        y[:, cut] += matmul(act[...], w_down[0, :, cut])
        dx[:, cut] += dot_nt(d_pre[...], w_up[0, cut, :])


def feed_forward(x, d_out, weights, bias, first_up, first_down, blocks):
    rows, width = x.shape
    hidden = weights.shape[2]
    whole = pl.BlockSpec((rows, width), lambda j: (0, 0))
    return pl.pallas_call(
        feed_kernel,
        grid=(blocks,),
        out_shape=(
            jax.ShapeDtypeStruct((rows, width), F32),
            jax.ShapeDtypeStruct((rows, width), F32),
            jax.ShapeDtypeStruct((blocks, width, hidden), BF16),
            jax.ShapeDtypeStruct((blocks, hidden, width), BF16),
            jax.ShapeDtypeStruct((blocks, 1, hidden), F32),
        ),
        in_specs=[
            whole,
            whole,
            pl.BlockSpec((1, width, hidden), lambda j: (first_up + j, 0, 0)),
            pl.BlockSpec((1, hidden, width), lambda j: (first_down + j, 0, 0)),
            pl.BlockSpec((1, 1, hidden), lambda j: (j, 0, 0)),
        ],
        out_specs=(
            whole,
            whole,
            pl.BlockSpec((1, width, hidden), lambda j: (j, 0, 0)),
            pl.BlockSpec((1, hidden, width), lambda j: (j, 0, 0)),
            pl.BlockSpec((1, 1, hidden), lambda j: (j, 0, 0)),
        ),
        scratch_shapes=[VMEM((width, rows), BF16), VMEM((rows, hidden), BF16), VMEM((rows, hidden), BF16)],
        compiler_params=pltpu.CompilerParams(
            dimension_semantics=("arbitrary",), vmem_limit_bytes=VMEM_LIMIT
        ),
        cost_estimate=pl.CostEstimate(
            flops=12 * blocks * rows * width * hidden,
            bytes_accessed=8 * blocks * width * hidden + 12 * rows * width,
            transcendentals=2 * blocks * rows * hidden,
        ),
        name="feed_forward",
    )(x, d_out, weights, weights, bias)


def any_gather(packed, small):
    return (
        lax.all_gather(packed, "fsdp", axis=1, tiled=True),
        lax.all_gather(small, "fsdp", axis=0, tiled=False),
    )


def any_reduce(parts, small):
    out = []
    for part in parts:
        mine = lax.psum_scatter(part, "fsdp", scatter_dimension=1, tiled=True)
        out.append(lax.psum(mine, "ctx"))
    return jnp.concatenate(out, axis=0), lax.psum(small, ("ctx", "fsdp"))


def any_forward(qkv, lengths):
    wide = lax.all_to_all(qkv, "ctx", split_axis=3, concat_axis=2, tiled=True)
    wide = jnp.swapaxes(wide, 0, 1)

    def one(item):
        rows, length = item
        mixed, levels = [], []

        def put(start, stop, part, level):
            mixed.append(part)
            levels.append(level)

        attend(rows[0], rows[1], rows[2], length, rows.shape[1], put)
        return mixed[0], levels[0]

    mixed, levels = lax.map(one, (wide, lengths))
    low = lax.all_to_all(mixed.astype(BF16), "ctx", split_axis=1, concat_axis=2, tiled=True)
    return low, wide, mixed, levels


def any_backward(dm_home, wide, mixed, levels, lengths):
    dm = lax.all_to_all(dm_home, "ctx", split_axis=2, concat_axis=1, tiled=True)

    def one(item):
        rows, part, level, upstream, length = item
        found = {}

        def put_query(start, stop, value):
            found[0] = value.astype(BF16)

        def put_key(start, stop, d_key, d_value):
            found[1], found[2] = d_key.T.astype(BF16), d_value.T.astype(BF16)

        attend_back(
            rows[0], rows[1], rows[2], part, level, upstream, length, rows.shape[1], put_query, put_key
        )
        return jnp.stack([found[0], found[1], found[2]])

    out = lax.map(one, (wide, mixed, levels, dm, lengths))
    out = lax.all_to_all(out, "ctx", split_axis=2, concat_axis=3, tiled=True)
    return jnp.swapaxes(out, 0, 1)


def body(
    routed,
    hidden_in,
    lengths,
    cotangent,
    w_qkv,
    bias_q,
    bias_v,
    w_out,
    bias_out,
    ln1_gain,
    ln1_bias,
    w_up,
    bias_up,
    w_down,
    bias_down,
    ln2_gain,
    ln2_bias,
):
    batch, seqs, slots, width = hidden_in.shape
    count = batch * seqs
    rows = count * slots
    shard = w_qkv.shape[0]
    shards = width // shard
    blocks = w_up.shape[1] // width

    up_parts = jnp.transpose(w_up.reshape(shard, shards, blocks, shard), (2, 0, 1, 3)).reshape(blocks, shard, width)
    packed = jnp.concatenate(
        [
            jnp.transpose(w_qkv.reshape(shard, 3, width), (1, 0, 2)),
            w_out[None],
            up_parts,
            w_down.reshape(blocks, shard, width),
        ],
        axis=0,
    )
    vectors = [bias_q, bias_v, bias_out, ln1_gain, ln1_bias, bias_down, ln2_gain, ln2_bias]
    small = jnp.concatenate([jnp.stack(vectors), bias_up.reshape(blocks, shard)], axis=0)
    small = jnp.pad(small, ((0, 16 - small.shape[0]), (0, 0)))
    weights, small_all = (gather_weights if routed else any_gather)(packed, small)
    small_all = jnp.transpose(small_all, (1, 0, 2)).reshape(16, width)
    full = small_all.astype(F32)
    full_q, full_v, full_bias_out, gain_one, shift_one, full_bias_down, gain_two, shift_two = [
        full[i] for i in range(8)
    ]
    full_up = small_all[8 : 8 + blocks].reshape(blocks, 1, width)

    flat_in = hidden_in.reshape(rows, width).astype(F32)
    normed = layer_norm(flat_in, gain_one, shift_one).astype(BF16)
    queries = (matmul(normed, weights[0]) + full_q).astype(BF16)
    key_rows = matmul(normed, weights[1]).astype(BF16)
    value_rows = (matmul(normed, weights[2]) + full_v).astype(BF16)
    qkv = jnp.stack([queries, key_rows, value_rows]).reshape(3, count, slots, width)
    flat_lengths = lengths.reshape(count)
    mixed_home, wide, mixed, levels = (attention_forward if routed else any_forward)(qkv, flat_lengths)
    mixed_low = mixed_home.reshape(rows, width)
    residual = flat_in + matmul(mixed_low, weights[3]) + full_bias_out
    normed2 = layer_norm(residual, gain_two, shift_two).astype(BF16)

    position = lax.axis_index("ctx") * slots + jnp.arange(slots, dtype=jnp.int32)
    filled = (position[None, :] < flat_lengths[:, None]).astype(F32).reshape(rows, 1)
    d_out = cotangent.reshape(rows, width).astype(F32) * filled
    d_branch = d_out.astype(BF16)
    fed, d_normed2, grad_up, grad_down, grad_bias_up = feed_forward(
        normed2, d_branch, weights, full_up, 4, 4 + blocks, blocks
    )
    output = (residual + fed + full_bias_down).astype(BF16)
    norm_pull_two = jax.vjp(layer_norm, residual, gain_two, shift_two)[1]
    d_resid_norm, grad_ln2_gain, grad_ln2_bias = norm_pull_two(d_normed2)
    d_residual = d_out + d_resid_norm
    d_attn = d_residual.astype(BF16)
    grad_out = dot_tn(mixed_low, d_attn).astype(BF16)
    d_mixed = dot_nt(d_attn, weights[3]).astype(BF16).reshape(count, slots, width)
    d_qkv = (attention_backward if routed else any_backward)(d_mixed, wide, mixed, levels, flat_lengths)
    d_qkv = d_qkv.reshape(3, rows, width)
    grad_qkv = jnp.stack([dot_tn(normed, d_qkv[i]).astype(BF16) for i in range(3)])
    d_normed = sum(dot_nt(d_qkv[i], weights[i]) for i in range(3))
    norm_pull_one = jax.vjp(layer_norm, flat_in, gain_one, shift_one)[1]
    d_input_norm, grad_ln1_gain, grad_ln1_bias = norm_pull_one(d_normed)
    grad_hidden = d_residual + d_input_norm

    small_grads = jnp.stack(
        [
            rows_sum(d_qkv[0]),
            rows_sum(d_qkv[2]),
            rows_sum(d_attn),
            grad_ln1_gain,
            grad_ln1_bias,
            jnp.sum(d_out, axis=0),
            grad_ln2_gain,
            grad_ln2_bias,
        ]
        + [grad_bias_up[j, 0] for j in range(blocks)]
        + [jnp.zeros((width,), F32)] * (8 - blocks)
    )
    parts = [grad_qkv, grad_out[None], grad_up, grad_down]
    if routed:
        sums, small_sums = reduce_gradients(parts, small_grads, 3)
    else:
        sums, small_sums = any_reduce(parts, small_grads)
    mine = lax.dynamic_slice_in_dim(small_sums, lax.axis_index("fsdp") * shard, shard, 1)
    sums = sums.astype(F32)
    out_qkv = jnp.transpose(sums[:3], (1, 0, 2)).reshape(shard, 3 * width)
    out_up = jnp.transpose(sums[4 : 4 + blocks].reshape(blocks, shard, shards, shard), (1, 2, 0, 3))
    return (
        output.reshape(hidden_in.shape),
        grad_hidden.reshape(hidden_in.shape),
        out_qkv,
        mine[0],
        mine[1],
        sums[3],
        mine[2],
        mine[3],
        mine[4],
        out_up.reshape(shard, blocks * width),
        mine[8 : 8 + blocks].reshape(blocks * shard),
        sums[4 + blocks :].reshape(blocks * shard, width),
        mine[5],
        mine[6],
        mine[7],
    )


def solution(mesh):
    row, vector, slot = P("fsdp", None), P("fsdp"), P(None, "fsdp", "ctx", None)
    routed = dict(mesh.shape) == {"ctx": 8, "fsdp": 4}
    return jax.shard_map(
        functools.partial(body, routed),
        mesh=mesh,
        in_specs=(
            slot, P(None, "fsdp"), slot, row, vector, vector, row, vector, vector, vector, row, vector, row, vector,
            vector, vector,
        ),
        out_specs=(
            slot, slot, row, vector, vector, row, vector, vector, vector, row, vector, row, vector, vector, vector,
        ),
        check_vma=False,
    )
```

time: 1430 us -> 545 us (0.38)
  waiting for transfers between devices: 850 us -> 0 us
  Pallas kernels: 0 us -> 414 us
  matrix products: 256 us -> 21.5 us
  blocking collectives: 123 us -> 0 us
  other arithmetic: 74.4 us -> 25.3 us
  local copies, waits for them, and re-layouts: 105 us -> 74.7 us
  between operations: 17.4 us -> 1.66 us
    reduce_scatter x6 -> x0, waiting for transfers between devices: 417 us -> none  [the longest x4 407 us: body(): lax.psum_scatter(as_sent(grad_totals), 'fsdp', scatter_dimension=0, tiled...]
    pallas_call x0 -> x5, Pallas kernels: none -> 414 us  [the longest x1 159 us: reduce_gradients(): pl.pallas_call(functools.partial(reduce_kernel, tuple(bounds), (0, 1, 3,...]
    all_gather x6 -> x0, waiting for transfers between devices: 371 us -> none  [the longest x1 144 us: body(): lax.all_gather(shards[7], 'fsdp', axis=0, tiled=True)]
    dot_general x36 -> x12, matrix products: 256 us -> 21.5 us  [the longest x4 7.88 us: dot_tn(): lax.dot_general(a, b, (((0,), (0,)), ((), ())), preferred_element_type=F32)]
    all_gather x9 -> x0, blocking collectives: 91.5 us -> none  [the longest x1 14.3 us: body(): lax.all_gather(shards[1], 'fsdp', axis=0, tiled=True)]
    psum x1 -> x0, waiting for transfers between devices: 60.1 us -> none  [body(): lax.psum(as_sent(scattered), 'ctx')]
    convert_element_type x38 -> x5, other arithmetic: 27.1 us -> 3.68 us  [the longest x1 3.07 us: body(): normed2 = layer_norm(residual, gain_two, shift_two).astype(BF16)]
    reshape x14 -> x7, local copies, waits for them, and re-layouts: 42.5 us -> 19.5 us  [the longest x2 6.89 us: body(): w_up.reshape(shard, shards, blocks, shard)]
  transfers between devices with their start and end apart: 13 -> 0, of which waited for: 11 -> 0; matrix products, arithmetic and copies ran while one was open for 21% -> 0% of each run, Pallas kernels for 0% -> 0%
where the time goes in v1:
time: 545 us; the launch traced here: 537 us
  Pallas kernels  414 us (76%)
  local copies, waits for them, and re-layouts  74.7 us (14%)
  other arithmetic  25.3 us (5%)
  matrix products  21.5 us (4%)
    pallas_call x1, Pallas kernels, reduce_gradients(): pl.pallas_call(functools.partial(reduce_kernel, tuple(bounds), (0, 1, 3,...  159 us
    pallas_call x1, Pallas kernels, gather_weights(): pl.pallas_call(functools.partial(gather_kernel, count, (0, 1, 2, 3, 5, 7,...  103 us
    pallas_call x1, Pallas kernels, attention_forward(): pl.pallas_call(attention_forward_kernel, out_shape=(jax.ShapeDtypeStruct(...  54.8 us
    pallas_call x1, Pallas kernels, attention_backward(): pl.pallas_call(attention_backward_kernel, out_shape=jax.ShapeDtypeStruct(...  53.8 us
    pallas_call x1, Pallas kernels, feed_forward(): pl.pallas_call(feed_kernel, grid=(blocks,), out_shape=(jax.ShapeDtypeStru...  43.3 us
    unnamed x78, local copies, waits for them, and re-layouts  15.8 us

profile of v1, /device:TPU:0, one launch (start us, length us, event | category | flops | bytes accessed | tf_op | source)
XLA Modules:
  0.0 537.4 jit_solution(13038575954705570233)
XLA Ops:
  0.6 4.5 reshape.423
  7.5 2.7 concatenate.19
  10.2 2.6 copy.36
  12.8 2.7 copy.37
  15.7 5.3 pad_maximum_fusion.src
  21.2 2.8 copy-done
  24.0 103.1 %gather_weights.1 = (bf16[12,4,2,2,2,2,16,1024]{7,6,5,4,3,2,1,0:T(8,128)(2,1)}, bf16[4,16,256]{2,1,0:T(8,128)(2,1)S(1)}) custom-call(bf16[12,2,2,2,2,16,1024]{6,5,4,3,2,1,0:T(8,128)(2,1)S(1)} %copy-done, bf16[16,256]{1,0:T(8,128)(2,1)S(1)} %pad.4.small), custom_call_target="tpu_custom_call" | custom-call | tf_op jit(solution)/shard_map/gather_weights/pallas_call | solution.py:205
  128.2 5.6 %fusion.21 = (bf16[1,4,2,2,2,2,16,1024]{7,6,5,4,3,2,1,0:T(8,128)(2,1)}, bf16[1,4,2,2,2,2,16,1024]{7,6,5,4,3,2,1,0:T(8,128)(2,1)S(1)}, bf16[1,4,2,2,2,2,16,1024]{...) fusion(bf16[12,4,2,2,2,2,16,1024]{7,6,5,4,3,2,1,0:T(8,128)(2,1)} %get-tuple-element.29), kind=kLoop, calls=%fused_computation.76 | loop fusion | bytes 16777216 | tf_op jit(solution)/shard_map/slice | solution.py:899
  141.0 54.8 %attention_forward.1 = (bf16[4,128,1024]{2,1,0:T(8,128)(2,1)}, bf16[4,3,1024,128]{3,2,1,0:T(8,128)(2,1)}, f32[4,1024,128]{2,1,0:T(8,128)}, f32[4,1024,128]{2,1,0:T(8,128)}) custom-call(bf16[3,4,128,1024]{3,2,1,0:T(8,128)(2,1)} %pad_maximum_fusion.2.qkv, s32[4]{0:T(128)} %reshape.425.lengths), custom_call_target="tpu_custom_call" | custom-call | tf_op jit(solution)/shard_map/attention_forward/pallas_call | solution.py:561
  195.8 3.3 fusion.25
  199.8 3.1 add_convert_fusion.1
  203.5 43.3 %feed_forward.1 = (f32[512,1024]{1,0:T(8,128)}, f32[512,1024]{1,0:T(8,128)}, bf16[4,1024,1024]{2,1,0:T(8,128)(2,1)}, bf16[4,1024,1024]{2,1,0:T(8,128)(2,1)}, f32[4,1,1024]{2,1,0:T(1,128)}) custom-call(bf16[512,1024]{1,0:T(8,128)(2,1)} %get-tuple-element.106.x, bf16[512,1024]{1,0:T(8,128)(2,1)} %get-tuple-element.107.d_out, ...), custom_call_target="tpu_custom_call" | custom-call | flops 25769803776 | bytes 39845888 | tf_op jit(solution)/shard_map/feed_forward/pallas_call | solution.py:748
  256.1 53.8 %attention_backward.1 = bf16[3,4,128,1024]{3,2,1,0:T(8,128)(2,1)} custom-call(bf16[4,128,1024]{2,1,0:T(8,128)(2,1)} %bitcast.169, bf16[4,3,1024,128]{3,2,1,0:T(8,128)(2,1)} %get-tuple-element.33.buf, f32[4,1024,128]{2,1,0:T(8,128)} %get-tuple-element.34.o, f32[4,1024,128]{2,1,0:T(8,128)} %get-tuple-element.35.levels, s32[4]{0:T(128)} %reshape.425.lengths), custom_call_target="tpu_custom_call" | custom-call | tf_op jit(solution)/shard_map/attention_backward/pallas_call | solution.py:693
  322.7 4.0 convolution_convert_fusion
  330.6 3.3 pad_maximum_fusion.1.refs_0_
  333.9 159.4 %reduce_gradients.1 = (bf16[12,2,2,2,2,16,1024]{6,5,4,3,2,1,0:T(8,128)(2,1)}, f32[5,16,1024]{2,1,0:T(8,128)}) custom-call(bf16[3,4,2,2,2,2,16,1024]{7,6,5,4,3,2,1,0:T(8,128)(2,1)} %pad_maximum_fusion.1.refs_0_, bf16[1,4,2,2,2,2,16,1024]{7,6,5,4,3,2,1,0:T(8,128)(2,1)} %bitcast.156, bf16[4,4,2,2,2,2,16,1024]{7,6,5,4,3,2,1,0:T(8,128)(2,1)} %bitcast.144, ...), custom_call_target="tpu_custom_call" | custom-call | tf_op jit(solution)/shard_map/reduce_gradients/pallas_call | solution.py:414
  493.3 6.8 %fusion.22 = (f32[4,2,2,2,2,16,1024]{6,5,4,3,2,1,0:T(8,128)}, f32[4,2,2,2,2,16,1024]{6,5,4,3,2,1,0:T(8,128)}) fusion(bf16[12,2,2,2,2,16,1024]{6,5,4,3,2,1,0:T(8,128)(2,1)} %get-tuple-element.39), kind=kLoop, calls=%fused_computation.77 | loop fusion | bytes 16777216 | tf_op jit(solution)/shard_map/slice | solution.py:959
  500.1 5.6 %reshape.439 = f32[4,256,4,256]{3,2,1,0:T(4,128)} reshape(f32[4,2,2,2,2,16,1024]{6,5,4,3,2,1,0:T(8,128)} %get-tuple-element.74) | data formatting | bytes 8388608 | tf_op jit(solution)/shard_map/reshape | solution.py:946
  505.7 7.0 %copy.41 = f32[256,4,4,256]{3,2,1,0:T(4,128)} copy(f32[256,4,4,256]{3,1,0,2:T(4,128)} %bitcast.141) | data formatting | bytes 8388608 | tf_op jit(solution)/shard_map/transpose | solution.py:946
  512.6 5.8 %reshape.440 = f32[256,4096]{1,0:T(8,128)} reshape(f32[256,4,4,256]{3,2,1,0:T(4,128)} %copy.41) | data formatting | bytes 8388608 | tf_op jit(solution)/shard_map/reshape | solution.py:957
  518.4 3.5 slice.186
  521.9 3.6 copy.40
  525.5 3.5 copy.42
  533.4 3.5 add_add_fusion.2
  (131 shorter events, 42.4 us)
Async XLA Ops:
  12.8 2.7 copy-start.8
  12.8 2.7 copy-start.24
  15.6 5.4 %copy-start.27 = (bf16[1024]{0:T(1024)(128)(2,1)S(1)}, bf16[1024]{0:T(1024)(128)(2,1)}, u32[]{:S(2)}) copy-start(bf16[1024]{0:T(1024)(128)(2,1)} %param.27) | copy-start | bytes 6148
  15.6 5.4 %copy-start.29 = (bf16[256]{0:T(256)(128)(2,1)S(1)}, bf16[256]{0:T(256)(128)(2,1)}, u32[]{:S(2)}) copy-start(bf16[256]{0:T(256)(128)(2,1)} %param.20) | copy-start | bytes 1540
  15.6 5.4 %copy-start.30 = (bf16[256]{0:T(256)(128)(2,1)S(1)}, bf16[256]{0:T(256)(128)(2,1)}, u32[]{:S(2)}) copy-start(bf16[256]{0:T(256)(128)(2,1)} %param.21) | copy-start | bytes 1540
  15.6 5.4 %copy-start.31 = (bf16[256]{0:T(256)(128)(2,1)S(1)}, bf16[256]{0:T(256)(128)(2,1)}, u32[]{:S(2)}) copy-start(bf16[256]{0:T(256)(128)(2,1)} %param.23) | copy-start | bytes 1540
  15.6 5.4 %copy-start.32 = (bf16[256]{0:T(256)(128)(2,1)S(1)}, bf16[256]{0:T(256)(128)(2,1)}, u32[]{:S(2)}) copy-start(bf16[256]{0:T(256)(128)(2,1)} %param.24) | copy-start | bytes 1540
  15.6 5.4 %copy-start.33 = (bf16[256]{0:T(256)(128)(2,1)S(1)}, bf16[256]{0:T(256)(128)(2,1)}, u32[]{:S(2)}) copy-start(bf16[256]{0:T(256)(128)(2,1)} %param.25) | copy-start | bytes 1540
  15.6 5.4 %copy-start.34 = (bf16[256]{0:T(256)(128)(2,1)S(1)}, bf16[256]{0:T(256)(128)(2,1)}, u32[]{:S(2)}) copy-start(bf16[256]{0:T(256)(128)(2,1)} %param.29) | copy-start | bytes 1540
  15.6 5.5 %copy-start.35 = (bf16[256]{0:T(256)(128)(2,1)S(1)}, bf16[256]{0:T(256)(128)(2,1)}, u32[]{:S(2)}) copy-start(bf16[256]{0:T(256)(128)(2,1)} %param.30) | copy-start | bytes 1540
  15.6 5.5 %copy-start.36 = (bf16[256]{0:T(256)(128)(2,1)S(1)}, bf16[256]{0:T(256)(128)(2,1)}, u32[]{:S(2)}) copy-start(bf16[256]{0:T(256)(128)(2,1)} %param.31) | copy-start | bytes 1540
  21.2 2.8 copy-start
  24.0 103.1 %copy-start.1 = (bf16[2,2,128,1024]{3,2,1,0:T(8,128)(2,1)S(1)}, bf16[2,2,128,1024]{3,2,1,0:T(8,128)(2,1)}, u32[]{:S(2)}) copy-start(bf16[2,2,128,1024]{3,2,1,0:T(8,128)(2,1)} %param.16) | copy-start | bytes 3145732
  128.2 8.9 %copy-start.18 = (bf16[2,2,128,1024]{3,2,1,0:T(8,128)(2,1)}, bf16[2,2,128,1024]{3,2,1,0:T(8,128)(2,1)S(1)}, u32[]{:S(2)}) copy-start(bf16[2,2,128,1024]{3,2,1,0:T(8,128)(2,1)S(1)} %fusion.8) | copy-start | bytes 3145732
  133.8 3.3 copy-start.15
  246.8 2.8 copy-start.12
  309.9 2.5 copy-start.16
  318.0 3.0 copy-start.5
  318.0 2.6 copy-start.2
  318.0 3.0 copy-start.25
  318.0 3.0 copy-start.7
  322.7 4.0 copy-start.19
  322.7 4.0 copy-start.23
  529.0 4.4 copy-start.4
  (13 other events, 22.1 us)

commit v2 on v1

v2 whole, which is shorter than its diff:
```python
import functools

import jax
import jax.numpy as jnp
from jax import lax
from jax.experimental import pallas as pl
from jax.experimental.pallas import tpu as pltpu
from jax.sharding import PartitionSpec as P

HEADS = 16
HEAD_DIM = 64
EPS = 1e-05
NEG_FILL = -1e30
MESH = pl.DeviceIdType.MESH
F32 = jnp.float32
BF16 = jnp.bfloat16
VMEM = pltpu.VMEM
DMA = pltpu.SemaphoreType.DMA
VMEM_LIMIT = 62 * 1024 * 1024
CHUNKS = 12


def layer_norm(inputs, ln_gain, ln_shift):
    center = jnp.mean(inputs, axis=-1, keepdims=True)
    centered = inputs - center
    spread = jnp.mean(centered * centered, axis=-1, keepdims=True)
    return centered * lax.rsqrt(spread + EPS) * ln_gain + ln_shift


def rows_sum(matrix):
    return jnp.sum(matrix.astype(F32), axis=0)


def matmul(left_side, right_side):
    return jnp.dot(left_side, right_side, preferred_element_type=F32)


def dot_nt(a, b):
    return lax.dot_general(a, b, (((1,), (1,)), ((), ())), preferred_element_type=F32)


def dot_tn(a, b):
    return lax.dot_general(a, b, (((0,), (0,)), ((), ())), preferred_element_type=F32)


def place():
    d = lax.axis_index("ctx")
    z = lax.axis_index("fsdp")
    return d, d // 4, lax.rem(d // 2, 2), lax.rem(d, 2), z


def remote(src, dst, send, recv, device):
    return pltpu.make_async_remote_copy(
        src_ref=src, dst_ref=dst, send_sem=send, recv_sem=recv, device_id=device, device_id_type=MESH
    )


def greet(devices):
    barrier = pltpu.get_barrier_semaphore()
    for device in devices:
        pl.semaphore_signal(barrier, inc=1, device_id=device, device_id_type=MESH)
    pl.semaphore_wait(barrier, len(devices))


def swap_rows(d):
    return (lambda s: 2 * s + d // 4), (lambda i: 4 * lax.rem(d, 2) + i)


def head_lanes(width):
    return lax.broadcasted_iota(jnp.int32, (1, width), 1) // HEAD_DIM


def attend(q, k, v, length, block, put):
    slots = k.shape[0]
    key_pos = lax.broadcasted_iota(jnp.int32, (1, slots), 1)
    bias = jnp.where(key_pos < length, 0.0, NEG_FILL).astype(F32)
    width = k.shape[1]
    lanes = head_lanes(width)
    causal = lax.broadcasted_iota(jnp.int32, (block, block), 1) <= lax.broadcasted_iota(
        jnp.int32, (block, block), 0
    )
    for start in range(0, slots, block):
        stop = start + block
        q_block = q[start:stop, :]
        sums, levels = None, None
        for head in range(width // HEAD_DIM):
            q_head = jnp.where(lanes == head, q_block, jnp.zeros_like(q_block)) * jnp.asarray(HEAD_DIM**-0.5, BF16)
            scores = dot_nt(q_head, k[:stop, :]) + bias[:, :stop]
            last = jnp.where(causal, scores[:, start:], NEG_FILL)
            top = jnp.max(last, axis=1, keepdims=True)
            if start:
                top = jnp.maximum(top, jnp.max(scores[:, :start], axis=1, keepdims=True))
                scores = jnp.concatenate([scores[:, :start], last], axis=1)
            else:
                scores = last
            weights = jnp.exp(scores - top)
            total = jnp.sum(weights, axis=1, keepdims=True)
            mixed = matmul(weights.astype(BF16), v[:stop, :]) / total
            level = top + jnp.log(total)
            sums = mixed if sums is None else jnp.where(lanes == head, mixed, sums)
            level = jnp.broadcast_to(level, mixed.shape)
            levels = level if levels is None else jnp.where(lanes == head, level, levels)
        put(start, stop, sums, levels)


def lanes_of(index, width=128):
    return pl.ds(pl.multiple_of(index * width, width), width)


def attend_back(q, k, v, o, levels, dm, length, block, put_query, put_key):
    slots, width = k.shape
    key_pos = lax.broadcasted_iota(jnp.int32, (1, slots), 1)
    bias = jnp.where(key_pos < length, 0.0, NEG_FILL).astype(F32)
    lanes = head_lanes(width)
    causal = lax.broadcasted_iota(jnp.int32, (block, block), 1) <= lax.broadcasted_iota(
        jnp.int32, (block, block), 0
    )
    scale = jnp.asarray(HEAD_DIM**-0.5, BF16)
    for start in range(0, slots, block):
        stop = start + block
        q_block = q[start:stop, :] * scale
        d_block = dm[start:stop, :]
        product = d_block.astype(F32) * o[start:stop, :].astype(F32)
        q_turned, d_turned = q_block.T, d_block.T
        d_query, d_keys, d_values = None, [], []
        for head in range(width // HEAD_DIM):
            here = lanes == head
            q_head = jnp.where(here, q_block, jnp.zeros_like(q_block))
            d_head = jnp.where(here, d_block, jnp.zeros_like(d_block))
            total = jnp.sum(jnp.where(here, product, 0.0), axis=1, keepdims=True)
            level = levels[start:stop, head * HEAD_DIM : head * HEAD_DIM + 1]
            scores = dot_nt(q_head, k[:stop, :]) + bias[:, :stop]
            last = jnp.where(causal, scores[:, start:], NEG_FILL)
            scores = jnp.concatenate([scores[:, :start], last], axis=1) if start else last
            weights = jnp.exp(scores - level)
            d_weight = dot_nt(d_head, v[:stop, :]) - total
            d_score = (weights * d_weight).astype(BF16)
            part = matmul(d_score, k[:stop, :])
            d_query = part if d_query is None else jnp.where(here, part, d_query)
            cut = slice(head * HEAD_DIM, (head + 1) * HEAD_DIM)
            d_values.append(matmul(d_turned[cut, :], weights.astype(BF16)))
            d_keys.append(matmul(q_turned[cut, :], d_score))
        put_query(start, stop, d_query * (HEAD_DIM**-0.5))
        put_key(start, stop, jnp.concatenate(d_keys, axis=0), jnp.concatenate(d_values, axis=0))


HIDDEN_BLOCKS = 4
UP, DOWN = 4, 5
GATHER_OFFSETS = (0, 1, 2, 3, 5, 7, 8)
GATHER_DELAY = 5


def flat_rows(value):
    return value.reshape((-1, value.shape[-1]))


def forward_kernel(
    w_qkv, w_out, w_up, w_down, small, hidden, cotangent, lengths,
    kept, full, home_hbm, normed_hbm, branch_hbm, buf_hbm, mine_hbm, level_hbm, mixed_hbm, residual_hbm,
    dx, g_up, g_down, g_bias, output,
    rows, normed, branch, buf, mine, level_out, mixed_low, residual, land, small_land, qkv, turned, total, stage_up, stage_down,
    ld, kd, vs, vr, zs, zr, xs, xr, cs, cr, hs, hr, es, er, ek, fs, fr, fk, us, ds_, os_,
):
    d, y, x, c, z = place()
    x_nb, y_nb, c_nb = (d + 2 - 4 * x, z), (d + 4 - 8 * y, z), (d + 1 - 2 * c, z)
    line = [(d, lax.rem(z + k, 4)) for k in (1, 2, 3)]
    width = full.shape[1]
    shard = width // 4
    half = normed.shape[0]
    pairs = mine.shape[1] // 128
    length = lengths[d // 4, lax.rem(d // 2, 2)]

    def own(chunk):
        copies = []
        if chunk < 3:
            copies.append((w_qkv.at[:, :, :, :, :, chunk * width : (chunk + 1) * width], land.at[chunk, z]))
        elif chunk == 3:
            copies.append((w_out, land.at[chunk, z]))
        elif chunk % 2 == UP % 2:
            j = (chunk - UP) // 2
            for i in range(4):
                low = i * width + j * shard
                copies.append(
                    (
                        w_up.at[:, :, :, :, :, low : low + shard],
                        land.at[chunk, z, :, :, :, :, :, i * shard : (i + 1) * shard],
                    )
                )
        else:
            copies.append((w_down.at[(chunk - DOWN) // 2], land.at[chunk, z]))
        return [pltpu.make_async_copy(a, b, ld.at[chunk, i]) for i, (a, b) in enumerate(copies)]

    for chunk in range(CHUNKS):
        for copy in own(chunk):
            copy.start()

    greet([(lax.rem(d + k, 8), z) for k in range(1, 8)] + line)

    goes, comes = swap_rows(d)

    def row_copy(ref, a, s):
        return remote(ref.at[s], rows.at[a, lax.rem(d, 4)], hs.at[a, s], hr.at[a, lax.rem(d, 4)], (goes(s), z))

    def row_keep(ref, a, s):
        return pltpu.make_async_copy(ref.at[s], rows.at[a, lax.rem(d, 4)], hs.at[a, s])

    def row_recv(a, i):
        ref = rows.at[a, i]
        return remote(ref, ref, hs.at[a, i], hr.at[a, i], c_nb)

    def rows_start(ref, a):
        for s in range(4):
            @pl.when(goes(s) == d)
            def _():
                row_keep(ref, a, s).start()

            @pl.when(goes(s) != d)
            def _():
                row_copy(ref, a, s).start()

    def rows_wait(ref, a):
        for s in range(4):
            @pl.when(goes(s) == d)
            def _():
                row_keep(ref, a, s).wait()

            @pl.when(goes(s) != d)
            def _():
                row_copy(ref, a, s).wait_send()

            @pl.when(comes(s) != d)
            def _():
                row_recv(a, s).wait_recv()

    def small_copy(k):
        return remote(small, small_land.at[z], vs.at[k], vr.at[k], line[k])

    def small_recv(k):
        return remote(small, small_land.at[lax.rem(z + 3 - k, 4)], vs.at[k], vr.at[k], line[k])

    def z_copy(chunk, k, down):
        ref = land.at[chunk, z + k if down else z - k, y, x, c]
        target = (d, z - 1) if down else (d, z + 1)
        return remote(ref, ref, zs.at[chunk, down, k], zr.at[chunk, down, k], target)

    def z_recv(chunk, k, down):
        ref = land.at[chunk, z + 1 + k if down else z - 1 - k, y, x, c]
        return remote(ref, ref, zs.at[chunk, down, k], zr.at[chunk, down, k], x_nb)

    def z_each(chunk, k, act_on):
        @pl.when((z < 3) & (z >= k))
        def _():
            act_on(z_copy(chunk, k, 0))

        @pl.when((z > 0) & (z + k <= 3))
        def _():
            act_on(z_copy(chunk, k, 1))

    def z_start(chunk, k):
        z_each(chunk, k, lambda copy: copy.start())

    def z_wait(chunk, k):
        @pl.when(z >= k + 1)
        def _():
            z_recv(chunk, k, 0).wait_recv()

        @pl.when(z + k + 1 <= 3)
        def _():
            z_recv(chunk, k, 1).wait_recv()

    def first(chunk, i, axis):
        ref = land.at[chunk, lax.rem(z + 1 + i, 4), y, x, c, axis]
        return remote(ref, ref, xs.at[chunk, 0, axis, i], xr.at[chunk, 0, axis, i], y_nb if axis else x_nb)

    def first_recv(chunk, i, axis):
        piece = lax.rem(z + 1 + i, 4)
        ref = land.at[chunk, piece, 1 - y, x, c, 1] if axis else land.at[chunk, piece, y, 1 - x, c, 0]
        return remote(ref, ref, xs.at[chunk, 0, axis, i], xr.at[chunk, 0, axis, i], y_nb if axis else x_nb)

    def second(chunk, i, axis):
        piece = lax.rem(z + 1 + i, 4)
        ref = land.at[chunk, piece, :, x, c, 1] if axis else land.at[chunk, piece, y, :, c, 0]
        return remote(ref, ref, xs.at[chunk, 1, axis, i], xr.at[chunk, 1, axis, i], x_nb if axis else y_nb)

    def second_recv(chunk, i, axis):
        piece = lax.rem(z + 1 + i, 4)
        ref = land.at[chunk, piece, :, 1 - x, c, 1] if axis else land.at[chunk, piece, 1 - y, :, c, 0]
        return remote(ref, ref, xs.at[chunk, 1, axis, i], xr.at[chunk, 1, axis, i], x_nb if axis else y_nb)

    def across(chunk, i, core):
        ref = land.at[chunk, lax.rem(z + 1 + i, 4), :, :, core]
        return remote(ref, ref, cs.at[chunk, i], cr.at[chunk, i], c_nb)

    def stage0(chunk):
        for index in range(CHUNKS):
            @pl.when(chunk == index)
            def _():
                for copy in own(index):
                    copy.wait()

        z_start(chunk, 0)

    def stage1(chunk):
        z_wait(chunk, 0)
        z_start(chunk, 1)

    def stage2(chunk):
        z_wait(chunk, 1)
        z_start(chunk, 2)

    def stage3(chunk):
        z_wait(chunk, 2)
        for i in range(3):
            for axis in range(2):
                first(chunk, i, axis).start()

    def stage4(chunk):
        for i in range(3):
            for axis in range(2):
                first_recv(chunk, i, axis).wait_recv()
        for i in range(3):
            for axis in range(2):
                second(chunk, i, axis).start()

    def stage5(chunk):
        for i in range(3):
            for axis in range(2):
                second_recv(chunk, i, axis).wait_recv()
        for i in range(3):
            across(chunk, i, c).start()

    def stage6(chunk):
        for i in range(3):
            across(chunk, i, 1 - c).wait_recv()
        for i in range(3):
            across(chunk, i, c).wait_send()
            for axis in range(2):
                first(chunk, i, axis).wait_send()
                second(chunk, i, axis).wait_send()
        for k in range(3):
            z_each(chunk, k, lambda copy: copy.wait_send())

    stages = [stage0, stage1, stage2, stage3, stage4, stage5, stage6]

    def tick(step):
        for index in reversed(range(len(stages))):
            begun = step - GATHER_OFFSETS[index]
            chunk = begun - jnp.where(begun >= 3, GATHER_DELAY, 0)

            @pl.when((begun >= 0) & ((begun < 3) | (begun >= 3 + GATHER_DELAY)) & (chunk < CHUNKS))
            def _():
                stages[index](chunk)

    results = [
        pltpu.make_async_copy(a, b, os_.at[i])
        for i, (a, b) in enumerate(
            [
                (rows.at[0], home_hbm), (normed, normed_hbm), (buf, buf_hbm), (mine, mine_hbm),
                (level_out, level_hbm), (mixed_low, mixed_hbm), (residual, residual_hbm), (branch, branch_hbm),
            ]
        )
    ]

    rows_start(hidden, 0)
    for k in range(3):
        small_copy(k).start()
    small_land[z] = small[...]

    @pl.loop(0, 4)
    def _(step):
        tick(step)

    for k in range(3):
        small_recv(k).wait_recv()
    for i in range(4):
        full[:, i * shard : (i + 1) * shard] = small_land[i].astype(F32)
    rows_wait(hidden, 0)

    def vector(index):
        return full[index : index + 1, :]

    @pl.loop(0, 4)
    def _(i):
        part = layer_norm(rows[0, i].astype(F32), vector(3), vector(4))
        normed[lanes_of(i), :] = part.astype(BF16)
        tick(4 + i)

    @pl.loop(8, 11)
    def _(step):
        tick(step)

    rows_start(cotangent, 1)
    results[0].start()
    results[1].start()
    for chunk in range(3):
        pltpu.make_async_copy(land.at[chunk], kept.at[chunk], kd.at[chunk]).start()
    tile = 256
    for u in range(3):
        @pl.loop(0, width // tile)
        def _(n):
            cut = lanes_of(n, tile)
            part = matmul(normed[...], flat_rows(land[u, :, :, :, :, :, :, cut]))
            if u != 1:
                part += full[u // 2 : u // 2 + 1, cut]
            qkv[u, :, cut] = part.astype(BF16)

        tick(11 + u)

    def send(h):
        return remote(
            qkv.at[:, :, lanes_of((1 - c) * pairs + h)],
            buf.at[:, lanes_of(c, half), lanes_of(h)], es.at[h], er.at[h], c_nb,
        )

    def keep(h):
        return pltpu.make_async_copy(
            qkv.at[:, :, lanes_of(c * pairs + h)], buf.at[:, lanes_of(c, half), lanes_of(h)], ek.at[h]
        )

    def recv(h):
        ref = buf.at[:, lanes_of(1 - c, half), lanes_of(h)]
        return remote(ref, ref, es.at[h], er.at[h], c_nb)

    def send_back(h):
        return remote(
            mine.at[lanes_of(1 - c, half), lanes_of(h)], mixed_low.at[:, lanes_of(c * pairs + h)],
            fs.at[h], fr.at[h], c_nb,
        )

    def keep_back(h):
        return pltpu.make_async_copy(
            mine.at[lanes_of(c, half), lanes_of(h)], mixed_low.at[:, lanes_of(c * pairs + h)], fk.at[h]
        )

    def recv_back(h):
        ref = mixed_low.at[:, lanes_of((1 - c) * pairs + h)]
        return remote(ref, ref, fs.at[h], fr.at[h], c_nb)

    @pl.loop(0, pairs)
    def _(h):
        send(h).start()
        keep(h).start()

    @pl.loop(0, pairs)
    def _(h):
        keep(h).wait()
        recv(h).wait_recv()
        cut = lanes_of(h)

        def put(start, stop, mixed, level):
            level_out[start:stop, cut] = level
            mine[start:stop, cut] = mixed.astype(BF16)

        attend(buf.at[0, :, cut], buf.at[1, :, cut], buf.at[2, :, cut], length, 256, put)
        send_back(h).start()
        keep_back(h).start()
        tick(14 + h)

    @pl.loop(0, pairs)
    def _(h):
        keep_back(h).wait()
        recv_back(h).wait_recv()
        send(h).wait_send()
        send_back(h).wait_send()

    for i in range(2, 6):
        results[i].start()

    act, d_pre, normed2 = qkv.at[0], qkv.at[1], qkv.at[2]

    @pl.loop(0, width // tile)
    def _(n):
        cut = lanes_of(n, tile)
        part = matmul(mixed_low[...], flat_rows(land[3, :, :, :, :, :, :, cut]))
        residual[:, cut] = flat_rows(rows[0, :, :, cut]).astype(F32) + part + full[2:3, cut]

    pltpu.make_async_copy(land.at[3], kept.at[3], kd.at[3]).start()
    tick(18)
    rows_wait(cotangent, 1)

    @pl.loop(0, 4)
    def _(i):
        cut = lanes_of(i)
        normed2[cut, :] = layer_norm(residual[cut, :], vector(6), vector(7)).astype(BF16)
        position = c * half + i * 128 + lax.broadcasted_iota(jnp.int32, (128, 1), 0)
        d_out = jnp.where(position < length, rows[1, i].astype(F32), 0.0)
        branch[cut, :] = d_out.astype(BF16)

    results[6].start()
    results[7].start()

    total[...] = jnp.zeros_like(total)
    dx[...] = jnp.zeros_like(dx)
    turned[...] = normed2[...].T

    def put_up(j, n):
        cut = lanes_of(n, tile)
        return pltpu.make_async_copy(stage_up.at[:, cut], g_up.at[j, :, cut], us.at[n])

    def put_down(j, n):
        cut = lanes_of(n, tile)
        return pltpu.make_async_copy(stage_down.at[cut, :], g_down.at[j, cut, :], ds_.at[n])

    @pl.loop(0, HIDDEN_BLOCKS)
    def _(j):
        up, down = UP + 2 * j, DOWN + 2 * j

        @pl.loop(0, width // tile)
        def _(n):
            cut = lanes_of(n, tile)

            @pl.when(j > 0)
            def _():
                put_up(j, n).wait()
                put_down(j, n).wait()

            pre = matmul(normed2[...], flat_rows(land[up, :, :, :, :, :, :, cut])) + full[pl.ds(8 + j, 1), cut]
            cumulative = 0.5 + 0.5 * lax.erf(pre * (0.5**0.5))
            active = (pre * cumulative).astype(BF16)
            act[:, cut] = active
            slope = cumulative + pre * (jnp.exp(-0.5 * pre * pre) * 0.3989422804014327)
            low = (dot_nt(branch[...], flat_rows(land[down, n])) * slope).astype(BF16)
            d_pre[:, cut] = low
            g_bias[pl.ds(j, 1), cut] = jnp.sum(low.astype(F32), axis=0, keepdims=True)
            stage_down[cut, :] = matmul(active.T, branch[...]).astype(BF16)
            stage_up[:, cut] = matmul(turned[...], low).astype(BF16)
            put_up(j, n).start()
            put_down(j, n).start()

        tick(19 + 2 * j)

        @pl.loop(0, width // tile)
        def _(n):
            cut = lanes_of(n, tile)
            total[:, cut] += matmul(act[...], flat_rows(land[down, :, :, :, :, :, :, cut]))
            dx[:, cut] += dot_nt(d_pre[...], flat_rows(land[up, n]))

        tick(20 + 2 * j)

    output[...] = (residual[...] + total[...] + full[5:6, :]).astype(BF16)
    for n in range(width // tile):
        put_up(0, n).wait()
        put_down(0, n).wait()
    for copy in results:
        copy.wait()
    for chunk in range(4):
        pltpu.make_async_copy(land.at[chunk], kept.at[chunk], kd.at[chunk]).wait()
    for k in range(3):
        small_copy(k).wait_send()


def forward(w_qkv, w_out, w_up, w_down, small, hidden, cotangent, lengths):
    shard, width = w_out.shape
    half = hidden.shape[0] * hidden.shape[1]
    slots, mine = 2 * half, width // 2
    pairs = mine // 128
    piece = (2, 2, 2, 2, shard // 16)
    vm, anywhere = pl.BlockSpec(memory_space=VMEM), pl.BlockSpec(memory_space=pl.ANY)
    shape = jax.ShapeDtypeStruct
    n = CHUNKS
    return pl.pallas_call(
        forward_kernel,
        out_shape=(
            shape((4, 4) + piece + (width,), BF16),
            shape((16, width), F32),
            shape(hidden.shape, BF16),
            shape((half, width), BF16),
            shape((half, width), BF16),
            shape((3, slots, mine), BF16),
            shape((slots, mine), BF16),
            shape((slots, mine), F32),
            shape((half, width), BF16),
            shape((half, width), F32),
            shape((half, width), F32),
            shape((HIDDEN_BLOCKS, width, width), BF16),
            shape((HIDDEN_BLOCKS, width, width), BF16),
            shape((8, width), F32),
            shape((half, width), BF16),
        ),
        in_specs=[anywhere] * 4 + [vm] + [anywhere] * 2 + [pl.BlockSpec(memory_space=pltpu.SMEM)],
        out_specs=(anywhere, vm) + (anywhere,) * 8 + (vm, anywhere, anywhere, vm, vm),
        scratch_shapes=[
            VMEM((2,) + hidden.shape, BF16),
            VMEM((half, width), BF16),
            VMEM((half, width), BF16),
            VMEM((3, slots, mine), BF16),
            VMEM((slots, mine), BF16),
            VMEM((slots, mine), F32),
            VMEM((half, width), BF16),
            VMEM((half, width), F32),
            VMEM((n, 4) + piece + (width,), BF16),
            VMEM((4,) + small.shape, BF16),
            VMEM((3, half, width), BF16),
            VMEM((width, half), BF16),
            VMEM((half, width), F32),
            VMEM((width, width), BF16),
            VMEM((width, width), BF16),
            DMA((n, 4)), DMA((4,)), DMA((3,)), DMA((3,)),
            DMA((n, 2, 3)), DMA((n, 2, 3)),
            DMA((n, 2, 2, 3)), DMA((n, 2, 2, 3)),
            DMA((n, 3)), DMA((n, 3)),
            DMA((2, 4)), DMA((2, 4)),
            DMA((pairs,)), DMA((pairs,)), DMA((pairs,)),
            DMA((pairs,)), DMA((pairs,)), DMA((pairs,)),
            DMA((4,)), DMA((4,)), DMA((8,)),
        ],
        compiler_params=pltpu.CompilerParams(
            collective_id=0, has_side_effects=True, vmem_limit_bytes=VMEM_LIMIT
        ),
        name="forward",
    )(
        w_qkv.reshape(piece + (3 * width,)),
        w_out.reshape(piece + (width,)),
        w_up.reshape(piece + (4 * width,)),
        w_down.reshape((HIDDEN_BLOCKS,) + piece + (width,)),
        small, hidden, cotangent, lengths,
    )


P_OFFSETS = (0, 1, 3, 5, 6, 7, 8, 9, 10, 11)
Q_OFFSETS = (0, 1, 3, 5, 7, 8, 9, 10, 11, 12)
LAST_STEP = 18
N_P, N_Q = 8, 4


def norm_back(x, upstream, gain):
    center = jnp.mean(x, axis=-1, keepdims=True)
    centered = x - center
    scale = lax.rsqrt(jnp.mean(centered * centered, axis=-1, keepdims=True) + EPS)
    hat = centered * scale
    t = upstream * gain
    back = scale * (t - jnp.mean(t, axis=-1, keepdims=True) - hat * jnp.mean(t * hat, axis=-1, keepdims=True))
    return back, jnp.sum(upstream * hat, axis=0, keepdims=True), jnp.sum(upstream, axis=0, keepdims=True)


def backward_kernel(
    kept, full, rows, normed, branch, buf, o_low, levels, mixed_low, residual, dx, g_up, g_down, g_bias, output,
    lengths,
    out, small_out, out_home, grad_home,
    acc, core_in, x_in, y_in, x_in2, y_in2, up_in, down_in, xq_in, yq_in, up_q, down_q, small_in,
    pair, pair_o, pair_l, dm, mine, turned, d_qkv, slot_a, slot_b, keep_f, work_f, d_attn, home_low, weight, stage,
    ls, cs, cr, s1, r1, s2, r2, zs, zr, gl, s3, r3, s4, r4, s5, r5, vs, vr, hs, hr,
    ps, ek, es, er, fk, fs, fr, ms, ws,
):
    d, y, x, c, z = place()
    x_nb, y_nb, c_nb = (d + 2 - 4 * x, z), (d + 4 - 8 * y, z), (d + 1 - 2 * c, z)
    line = [(d, lax.rem(z + k, 4)) for k in (1, 2, 3)]
    width = full.shape[1]
    half = d_attn.shape[0]
    pairs = dm.shape[1] // 128
    length = lengths[d // 4, lax.rem(d // 2, 2)]
    tile = 256

    def local(src, dst, sem):
        return pltpu.make_async_copy(src, dst, sem)

    loads = [
        local(residual, keep_f, ms.at[0]), local(dx, work_f, ms.at[1]), local(branch, slot_b, ms.at[2]),
        local(mixed_low, slot_a, ms.at[3]),
    ]
    for copy in loads:
        copy.start()
    local(kept.at[3], weight, ws).start()
    greet([(lax.rem(d + k, 8), z) for k in range(1, 8)] + line)

    comes, goes = swap_rows(d)

    def row_copy(src, dst, a, i):
        return remote(src(i), dst.at[d // 2], hs.at[a, i], hr.at[a, d // 2], (goes(i), z))

    def row_keep(src, dst, a, i):
        return local(src(i), dst.at[d // 2], hs.at[a, i])

    def row_recv(dst, a, s):
        return remote(dst.at[s], dst.at[s], hs.at[a, s], hr.at[a, s], c_nb)

    def rows_start(src, dst, a):
        for i in range(4):
            @pl.when(goes(i) == d)
            def _():
                row_keep(src, dst, a, i).start()

            @pl.when(goes(i) != d)
            def _():
                row_copy(src, dst, a, i).start()

    def rows_wait(src, dst, a):
        for i in range(4):
            @pl.when(goes(i) == d)
            def _():
                row_keep(src, dst, a, i).wait()

            @pl.when(goes(i) != d)
            def _():
                row_copy(src, dst, a, i).wait_send()

            @pl.when(comes(i) != d)
            def _():
                row_recv(dst, a, i).wait_recv()

    def output_block(i):
        return output.at[i]

    def grad_block(i):
        return home_low.at[i * 128 : (i + 1) * 128, :]

    def load(ref, chunk, slot):
        return local(ref.at[chunk, :, :, :, c], acc.at[slot], ls.at[slot])

    def core_send(ref, slot, into):
        return remote(ref, core_in.at[into], cs.at[slot], cr.at[slot], c_nb)

    def down_send(k):
        return core_send(g_down.at[k, :, :, :, 1 - c], k, k)

    def up_send(k):
        return core_send(g_up.at[k, :, :, :, 1 - c], N_P + k, 5 + k)

    def stage_send(slot, into):
        return core_send(stage, slot, into)

    def core_add(slot, into):
        stage_send(slot, into).wait_recv()
        for piece in range(4):
            acc[slot, piece] += core_in[into, piece]

    def x1(k):
        return remote(acc.at[k, :, :, 1 - x, 0], x_in.at[k], s1.at[k, 0], r1.at[k, 0], x_nb)

    def y1(k):
        return remote(acc.at[k, :, 1 - y, :, 1], y_in.at[k], s1.at[k, 1], r1.at[k, 1], y_nb)

    def y2(k):
        return remote(acc.at[k, :, 1 - y, x, 0], y_in2.at[k], s2.at[k, 0], r2.at[k, 0], y_nb)

    def x2(k):
        return remote(acc.at[k, :, y, 1 - x, 1], x_in2.at[k], s2.at[k, 1], r2.at[k, 1], x_nb)

    def qx1(k):
        return remote(acc.at[N_P + k, z, :, 1 - x, 0], xq_in.at[k, 0:2], s1.at[N_P + k, 0], r1.at[N_P + k, 0], x_nb)

    def qy1(k):
        return remote(acc.at[N_P + k, z, 1 - y, :, 1], yq_in.at[k, 0:2], s1.at[N_P + k, 1], r1.at[N_P + k, 1], y_nb)

    def qy2(k):
        return remote(acc.at[N_P + k, z, 1 - y, x, 0], yq_in.at[k, 2], s2.at[N_P + k, 0], r2.at[N_P + k, 0], y_nb)

    def qx2(k):
        return remote(acc.at[N_P + k, z, y, 1 - x, 1], xq_in.at[k, 2], s2.at[N_P + k, 1], r2.at[N_P + k, 1], x_nb)

    def p_up(k, i):
        return remote(acc.at[k, z + 3 - i, y, x], up_in.at[k, i], zs.at[k, 0, i], zr.at[k, 0, i], (d, z + 1))

    def p_down(k, i):
        return remote(acc.at[k, z - 3 + i, y, x], down_in.at[k, i], zs.at[k, 1, i], zr.at[k, 1, i], (d, z - 1))

    def q_up(k, i):
        return remote(
            acc.at[N_P + k, z + 3 - i], up_q.at[k, i], zs.at[N_P + k, 0, i], zr.at[N_P + k, 0, i], (d, z + 1)
        )

    def q_down(k, i):
        return remote(
            acc.at[N_P + k, z - 3 + i], down_q.at[k, i], zs.at[N_P + k, 1, i], zr.at[N_P + k, 1, i], (d, z - 1)
        )

    def z_each(up, down, k, i, act):
        @pl.when((z < 3) & (z <= i))
        def _():
            act(up(k, i))

        @pl.when((z > 0) & (z >= 3 - i))
        def _():
            act(down(k, i))

    def z_send(up, down, k, i):
        z_each(up, down, k, i, lambda copy: copy.start())

    def z_add(up_ref, down_ref, k, base, i, add_up, add_down):
        @pl.when((z >= 1) & (z - 1 <= i))
        def _():
            ref = up_ref.at[k, i]
            remote(ref, ref, zs.at[base + k, 0, i], zr.at[base + k, 0, i], c_nb).wait_recv()
            add_up(k, i)

        @pl.when((z <= 2) & (z + 1 >= 3 - i))
        def _():
            ref = down_ref.at[k, i]
            remote(ref, ref, zs.at[base + k, 1, i], zr.at[base + k, 1, i], c_nb).wait_recv()
            add_down(k, i)

    def p_add_up(k, i):
        acc[k, z + 2 - i, y, x] += up_in[k, i]

    def p_add_down(k, i):
        acc[k, z - 2 + i, y, x] += down_in[k, i]

    def q_add_up(k, i):
        acc[N_P + k, z + 2 - i] += up_q[k, i]

    def q_add_down(k, i):
        acc[N_P + k, z - 2 + i] += down_q[k, i]

    def g0(k):
        return local(acc.at[k, z, y, x], out.at[k, y, x, c], gl.at[k])

    def g1(k, axis):
        return remote(
            acc.at[k, z, y, x, axis], out.at[k, y, x, c, axis], s3.at[k, axis], r3.at[k, axis],
            y_nb if axis else x_nb,
        )

    def g1_recv(k, axis):
        ref = out.at[k, 1 - y, x, c, 1] if axis else out.at[k, y, 1 - x, c, 0]
        return remote(ref, ref, s3.at[k, axis], r3.at[k, axis], y_nb if axis else x_nb)

    def g2(k, axis):
        ref = out.at[k, :, x, c, 1] if axis else out.at[k, y, :, c, 0]
        return remote(ref, ref, s4.at[k, axis], r4.at[k, axis], x_nb if axis else y_nb)

    def g2_recv(k, axis):
        ref = out.at[k, :, 1 - x, c, 1] if axis else out.at[k, 1 - y, :, c, 0]
        return remote(ref, ref, s4.at[k, axis], r4.at[k, axis], x_nb if axis else y_nb)

    def g3(k, core):
        ref = out.at[k, :, :, core]
        return remote(ref, ref, s5.at[k], r5.at[k], c_nb)

    def spread1(k):
        g0(k).start()
        g1(k, 0).start()
        g1(k, 1).start()

    def spread2(k):
        g0(k).wait()
        for axis in range(2):
            g1_recv(k, axis).wait_recv()
        for axis in range(2):
            g2(k, axis).start()

    def spread3(k):
        for axis in range(2):
            g2_recv(k, axis).wait_recv()
        g3(k, c).start()

    def spread4(k):
        g3(k, 1 - c).wait_recv()
        g3(k, c).wait_send()
        for axis in range(2):
            g1(k, axis).wait_send()
            g2(k, axis).wait_send()

    def p0(k):
        @pl.when(k < 4)
        def _():
            down_send(k).start()
            load(g_down, k, k).start()

    def p1(k):
        @pl.when(k < 4)
        def _():
            load(g_down, k, k).wait()

        core_add(k, jnp.where(k >= 5, k - 5, k))
        x1(k).start()
        y1(k).start()

    def p2(k):
        x1(k).wait_recv()
        y1(k).wait_recv()
        acc[k, :, :, x, 0] += x_in[k]
        acc[k, :, y, :, 1] += y_in[k]
        y2(k).start()
        x2(k).start()

    def p3(k):
        y2(k).wait_recv()
        x2(k).wait_recv()
        acc[k, :, y, x, 0] += y_in2[k]
        acc[k, :, y, x, 1] += x_in2[k]
        z_send(p_up, p_down, k, 0)

    def p4(k):
        z_add(up_in, down_in, k, 0, 0, p_add_up, p_add_down)
        z_send(p_up, p_down, k, 1)

    def p5(k):
        z_add(up_in, down_in, k, 0, 1, p_add_up, p_add_down)
        z_send(p_up, p_down, k, 2)

    def p6(k):
        z_add(up_in, down_in, k, 0, 2, p_add_up, p_add_down)
        spread1(k)

    def p9(k):
        spread4(k)

        @pl.when(k < 4)
        def _():
            down_send(k).wait_send()

        for copy in (x1(k), y1(k), x2(k), y2(k)):
            copy.wait_send()
        for i in range(3):
            z_each(p_up, p_down, k, i, lambda copy: copy.wait_send())

    def q0(k):
        up_send(k).start()
        load(g_up, k, N_P + k).start()

    def q1(k):
        load(g_up, k, N_P + k).wait()
        core_add(N_P + k, 5 + k)
        z_send(q_up, q_down, k, 0)

    def q2(k):
        z_add(up_q, down_q, k, N_P, 0, q_add_up, q_add_down)
        z_send(q_up, q_down, k, 1)

    def q3(k):
        z_add(up_q, down_q, k, N_P, 1, q_add_up, q_add_down)
        z_send(q_up, q_down, k, 2)

    def q4(k):
        z_add(up_q, down_q, k, N_P, 2, q_add_up, q_add_down)
        qx1(k).start()
        qy1(k).start()

    def q5(k):
        qx1(k).wait_recv()
        qy1(k).wait_recv()
        acc[N_P + k, z, :, x, 0] += xq_in[k, 0:2]
        acc[N_P + k, z, y, :, 1] += yq_in[k, 0:2]
        qy2(k).start()
        qx2(k).start()

    def q6(k):
        qy2(k).wait_recv()
        qx2(k).wait_recv()
        acc[N_P + k, z, y, x, 0] += yq_in[k, 2]
        acc[N_P + k, z, y, x, 1] += xq_in[k, 2]
        spread1(N_P + k)

    def q9(k):
        spread4(N_P + k)
        up_send(k).wait_send()
        for copy in (qx1(k), qy1(k), qx2(k), qy2(k)):
            copy.wait_send()
        for i in range(3):
            z_each(q_up, q_down, k, i, lambda copy: copy.wait_send())

    p_stages = [p0, p1, p2, p3, p4, p5, p6, spread2, spread3, p9]
    q_stages = [
        q0, q1, q2, q3, q4, q5, q6, lambda k: spread2(N_P + k), lambda k: spread3(N_P + k), q9,
    ]

    def tick(step):
        step = jnp.asarray(step, jnp.int32)
        for index in reversed(range(10)):
            q_begun = step - Q_OFFSETS[index]

            @pl.when((q_begun == 0) | ((q_begun >= 0) & (q_begun < 2 * N_Q - 1) & (lax.rem(q_begun + 64, 2) == 1)))
            def _():
                q_stages[index]((q_begun + 1) // 2)

            begun = step - P_OFFSETS[index]

            @pl.when((begun >= 0) & (begun < N_P))
            def _():
                p_stages[index](begun)

    tick(0)
    rows_start(output_block, out_home, 0)

    for copy in loads:
        copy.wait()
    small_out[0] = jnp.zeros_like(small_out[0])
    small_out[0, 8:12, :] = g_bias[0:4, :]

    def add_small(index, value):
        small_out[0, index : index + 1, :] += value

    @pl.loop(0, 4)
    def _(i):
        cut = lanes_of(i)
        d_out = slot_b[cut, :].astype(F32)
        back, gain, shift = norm_back(keep_f[cut, :], work_f[cut, :], full[6:7, :])
        d_residual = d_out + back
        keep_f[cut, :] = d_residual
        low = d_residual.astype(BF16)
        d_attn[cut, :] = low
        add_small(2, jnp.sum(low.astype(F32), axis=0, keepdims=True))
        add_small(5, jnp.sum(d_out, axis=0, keepdims=True))
        add_small(6, gain)
        add_small(7, shift)

    tick(1)

    def put_gradient(slot, cut, value):
        value = value.astype(BF16).reshape(4, 2, 2, 2, 2, 16, tile)
        even, odd = value[:, :, :, 0], value[:, :, :, 1]
        first = c == 0
        acc[slot, :, :, :, :, :, cut] = jnp.where(first, even, odd)
        stage[:, :, :, :, :, cut] = jnp.where(first, odd, even)

    for i in range(2):
        d_qkv[0, :, i * half : (i + 1) * half] = slot_a[:, i * half : (i + 1) * half].T

    @pl.loop(0, width // tile)
    def _(n):
        cut = lanes_of(n, tile)
        halves = [matmul(d_qkv[0, :, i * half : (i + 1) * half], d_attn[:, cut]) for i in range(2)]
        put_gradient(4, cut, jnp.concatenate(halves, axis=0))

    stage_send(4, 4).start()
    local(kept.at[3], weight, ws).wait()

    @pl.loop(0, width // tile)
    def _(n):
        cut = lanes_of(n, tile)
        home_low[:, cut] = dot_nt(d_attn[...], flat_rows(weight[n])).astype(BF16)

    local(kept.at[0], weight, ws).start()
    home_rows = local(rows, slot_b, ms.at[2])
    normed_rows = local(normed, slot_a, ms.at[3])
    home_rows.start()
    normed_rows.start()

    def pair_loads(h):
        slot = lax.rem(h, 2)
        cut = lanes_of(h)
        return [
            local(buf.at[:, :, cut], pair.at[slot], ps.at[slot, 0]),
            local(o_low.at[:, cut], pair_o.at[slot], ps.at[slot, 1]),
            local(levels.at[:, cut], pair_l.at[slot], ps.at[slot, 2]),
        ]

    def send(h):
        return remote(
            home_low.at[:, lanes_of((1 - c) * pairs + h)], dm.at[lanes_of(c, half), lanes_of(h)],
            es.at[h], er.at[h], c_nb,
        )

    def keep(h):
        return local(home_low.at[:, lanes_of(c * pairs + h)], dm.at[lanes_of(c, half), lanes_of(h)], ek.at[h])

    def recv(h):
        ref = dm.at[lanes_of(1 - c, half), lanes_of(h)]
        return remote(ref, ref, es.at[h], er.at[h], c_nb)

    def send_back(h):
        return remote(
            mine.at[lax.rem(h, 2), :, lanes_of(1 - c, half), :], d_qkv.at[:, :, lanes_of(c * pairs + h)],
            fs.at[h], fr.at[h], c_nb,
        )

    def keep_back(h):
        return local(
            mine.at[lax.rem(h, 2), :, lanes_of(c, half), :], d_qkv.at[:, :, lanes_of(c * pairs + h)], fk.at[h]
        )

    def recv_back(h):
        ref = d_qkv.at[:, :, lanes_of((1 - c) * pairs + h)]
        return remote(ref, ref, fs.at[h], fr.at[h], c_nb)

    for copy in pair_loads(0):
        copy.start()

    @pl.loop(0, pairs)
    def _(h):
        send(h).start()
        keep(h).start()

    tick(2)

    @pl.loop(0, pairs)
    def _(h):
        for copy in pair_loads(h):
            copy.wait()

        @pl.when(h + 1 < pairs)
        def _():
            for copy in pair_loads(h + 1):
                copy.start()

        keep(h).wait()
        recv(h).wait_recv()

        @pl.when(h >= 2)
        def _():
            send_back(h - 2).wait_send()
            keep_back(h - 2).wait()

        turned[...] = jnp.zeros_like(turned)
        slot = lax.rem(h, 2)

        def put_query(start, stop, value):
            mine[slot, 0, start:stop, :] = value.astype(BF16)

        def put_key(start, stop, d_key, d_value):
            turned[0, :, :stop] += d_key
            turned[1, :, :stop] += d_value

        attend_back(
            pair.at[slot, 0], pair.at[slot, 1], pair.at[slot, 2], pair_o.at[slot], pair_l.at[slot],
            dm.at[:, lanes_of(h)], length, 256, put_query, put_key,
        )
        mine[slot, 1] = turned[0].T.astype(BF16)
        mine[slot, 2] = turned[1].T.astype(BF16)
        send_back(h).start()
        keep_back(h).start()
        tick(jnp.where(lax.rem(h, 2) == 1, 3 + h // 2, -1000))

    @pl.loop(0, pairs)
    def _(h):
        recv_back(h).wait_recv()
        send(h).wait_send()

    for h in range(pairs - 2, pairs):
        send_back(h).wait_send()
        keep_back(h).wait()
    home_rows.wait()
    normed_rows.wait()

    dm[...] = slot_a[...].T
    for u in range(3):
        stage_send(4 + u, 4 if u == 0 else u - 1).wait_send()

        @pl.loop(0, width // tile)
        def _(n):
            cut = lanes_of(n, tile)
            put_gradient(5 + u, cut, matmul(dm[...], d_qkv[u, :, cut]))

        stage_send(5 + u, u).start()
        local(kept.at[u], weight, ws).wait()

        @pl.loop(0, width // tile)
        def _(n):
            cut = lanes_of(n, tile)
            part = dot_nt(d_qkv[u], flat_rows(weight[n]))
            work_f[:, cut] = part if u == 0 else work_f[:, cut] + part

        if u < 2:
            local(kept.at[u + 1], weight, ws).start()
        if u != 1:
            add_small(u // 2, jnp.sum(d_qkv[u].astype(F32), axis=0, keepdims=True))
        tick(5 + u)

    @pl.loop(0, 4)
    def _(i):
        cut = lanes_of(i)
        back, gain, shift = norm_back(slot_b[cut, :].astype(F32), work_f[cut, :], full[3:4, :])
        home_low[cut, :] = (keep_f[cut, :] + back).astype(BF16)
        add_small(3, gain)
        add_small(4, shift)

    rows_start(grad_block, grad_home, 1)

    def vector_copy(step):
        nb = (c_nb, x_nb, y_nb)[step]
        return remote(small_out.at[step], small_in.at[step], vs.at[step], vr.at[step], nb)

    for step in range(3):
        vector_copy(step).start()
        tick(8 + step)
        vector_copy(step).wait()
        small_out[step + 1] = small_out[step] + small_in[step]
    copies = [remote(small_out.at[3], small_in.at[3 + k], vs.at[3 + k], vr.at[3 + k], line[k]) for k in range(3)]
    for copy in copies:
        copy.start()

    @pl.loop(11, LAST_STEP + 1)
    def _(step):
        tick(step)

    for copy in copies:
        copy.wait()
    small_out[4] = small_out[3] + small_in[3] + small_in[4] + small_in[5]
    stage_send(7, 2).wait_send()
    rows_wait(output_block, out_home, 0)
    rows_wait(grad_block, grad_home, 1)


def backward(
    kept, full, rows, normed, branch, buf, o_low, levels, mixed_low, residual, dx, g_up, g_down, g_bias, output, lengths
):
    half, width = normed.shape
    slots, lanes = o_low.shape
    pairs = lanes // 128
    piece, n = 16, N_P + N_Q
    vm, anywhere = pl.BlockSpec(memory_space=VMEM), pl.BlockSpec(memory_space=pl.ANY)
    shape = jax.ShapeDtypeStruct
    block = (4, 2, 2, 2, 2, piece, width)
    home = (4, half // 4, width)
    vectors = (16, width)
    out, small_out, out_home, grad_home = pl.pallas_call(
        backward_kernel,
        out_shape=(
            shape((n, 2, 2, 2, 2, piece, width), BF16),
            shape((5,) + vectors, F32),
            shape(home, BF16),
            shape(home, BF16),
        ),
        in_specs=[anywhere, vm] + [anywhere] * 11 + [vm, anywhere, pl.BlockSpec(memory_space=pltpu.SMEM)],
        out_specs=(anywhere, vm, anywhere, anywhere),
        scratch_shapes=[
            VMEM((n, 4, 2, 2, 2, piece, width), BF16),
            VMEM((9, 4, 2, 2, 2, piece, width), BF16),
            VMEM((N_P, 4, 2, piece, width), BF16),
            VMEM((N_P, 4, 2, piece, width), BF16),
            VMEM((N_P, 4, piece, width), BF16),
            VMEM((N_P, 4, piece, width), BF16),
            VMEM((N_P, 3, 2, piece, width), BF16),
            VMEM((N_P, 3, 2, piece, width), BF16),
            VMEM((N_Q, 3, piece, width), BF16),
            VMEM((N_Q, 3, piece, width), BF16),
            VMEM((N_Q, 3, 2, 2, 2, piece, width), BF16),
            VMEM((N_Q, 3, 2, 2, 2, piece, width), BF16),
            VMEM((6,) + vectors, F32),
            VMEM((2, 3, slots, 128), BF16),
            VMEM((2, slots, 128), BF16),
            VMEM((2, slots, 128), F32),
            VMEM((slots, lanes), BF16),
            VMEM((2, 3, slots, 128), BF16),
            VMEM((2, 128, slots), F32),
            VMEM((3, half, width), BF16),
            VMEM((half, width), BF16),
            VMEM((half, width), BF16),
            VMEM((half, width), F32),
            VMEM((half, width), F32),
            VMEM((half, width), BF16),
            VMEM((half, width), BF16),
            VMEM(block, BF16),
            VMEM((4, 2, 2, 2, piece, width), BF16),
            DMA((n,)), DMA((n,)), DMA((n,)),
            DMA((n, 2)), DMA((n, 2)), DMA((n, 2)), DMA((n, 2)),
            DMA((n, 2, 3)), DMA((n, 2, 3)), DMA((n,)),
            DMA((n, 2)), DMA((n, 2)), DMA((n, 2)), DMA((n, 2)),
            DMA((n,)), DMA((n,)), DMA((6,)), DMA((6,)),
            DMA((2, 4)), DMA((2, 4)),
            DMA((2, 3)),
            DMA((pairs,)), DMA((pairs,)), DMA((pairs,)),
            DMA((pairs,)), DMA((pairs,)), DMA((pairs,)),
            DMA((4,)), DMA,
        ],
        compiler_params=pltpu.CompilerParams(
            collective_id=1, has_side_effects=True, vmem_limit_bytes=VMEM_LIMIT
        ),
        name="backward",
    )(
        kept, full, rows.reshape(half, width), normed, branch, buf, o_low, levels, mixed_low, residual, dx,
        g_up.reshape((N_Q,) + block), g_down.reshape((4,) + block), g_bias, output.reshape(home), lengths,
    )
    return out.reshape(n, 16 * piece, width), small_out[4], out_home, grad_home


def feed_kernel(x, d_out, w_up, w_down, bias, y, dx, g_up, g_down, g_bias, x_turned, act, d_pre):
    tile = 256
    hidden = w_up.shape[2]

    @pl.when(pl.program_id(0) == 0)
    def _():
        y[...] = jnp.zeros_like(y)
        dx[...] = jnp.zeros_like(dx)
        x_turned[...] = x[...].T

    @pl.loop(0, hidden // tile)
    def _(n):
        cut = pl.ds(pl.multiple_of(n * tile, tile), tile)
        pre = matmul(x[...], w_up[0, :, cut]) + bias[0, :, cut].astype(F32)
        cumulative = 0.5 + 0.5 * lax.erf(pre * (0.5**0.5))
        active = (pre * cumulative).astype(BF16)
        act[:, cut] = active
        slope = cumulative + pre * (jnp.exp(-0.5 * pre * pre) * 0.3989422804014327)
        back = dot_nt(d_out[...], w_down[0, cut, :]) * slope
        low = back.astype(BF16)
        d_pre[:, cut] = low
        g_bias[0, :, cut] = jnp.sum(low.astype(F32), axis=0, keepdims=True)
        g_down[0, cut, :] = matmul(active.T, d_out[...]).astype(BF16)
        g_up[0, :, cut] = matmul(x_turned[...], low).astype(BF16)

    @pl.loop(0, y.shape[1] // tile)
    def _(n):
        cut = pl.ds(pl.multiple_of(n * tile, tile), tile)
        y[:, cut] += matmul(act[...], w_down[0, :, cut])
        dx[:, cut] += dot_nt(d_pre[...], w_up[0, cut, :])


def feed_forward(x, d_out, weights, bias, first_up, first_down, blocks):
    rows, width = x.shape
    hidden = weights.shape[2]
    whole = pl.BlockSpec((rows, width), lambda j: (0, 0))
    return pl.pallas_call(
        feed_kernel,
        grid=(blocks,),
        out_shape=(
            jax.ShapeDtypeStruct((rows, width), F32),
            jax.ShapeDtypeStruct((rows, width), F32),
            jax.ShapeDtypeStruct((blocks, width, hidden), BF16),
            jax.ShapeDtypeStruct((blocks, hidden, width), BF16),
            jax.ShapeDtypeStruct((blocks, 1, hidden), F32),
        ),
        in_specs=[
            whole,
            whole,
            pl.BlockSpec((1, width, hidden), lambda j: (first_up + j, 0, 0)),
            pl.BlockSpec((1, hidden, width), lambda j: (first_down + j, 0, 0)),
            pl.BlockSpec((1, 1, hidden), lambda j: (j, 0, 0)),
        ],
        out_specs=(
            whole,
            whole,
            pl.BlockSpec((1, width, hidden), lambda j: (j, 0, 0)),
            pl.BlockSpec((1, hidden, width), lambda j: (j, 0, 0)),
            pl.BlockSpec((1, 1, hidden), lambda j: (j, 0, 0)),
        ),
        scratch_shapes=[VMEM((width, rows), BF16), VMEM((rows, hidden), BF16), VMEM((rows, hidden), BF16)],
        compiler_params=pltpu.CompilerParams(
            dimension_semantics=("arbitrary",), vmem_limit_bytes=VMEM_LIMIT
        ),
        cost_estimate=pl.CostEstimate(
            flops=12 * blocks * rows * width * hidden,
            bytes_accessed=8 * blocks * width * hidden + 12 * rows * width,
            transcendentals=2 * blocks * rows * hidden,
        ),
        name="feed_forward",
    )(x, d_out, weights, weights, bias)


def finish_kernel(sums, qkv, out, up, down):
    width = out.shape[1]
    shard = width // 4
    out[...] = sums[4].astype(F32)
    for i in range(3):
        qkv[:, i * width : (i + 1) * width] = sums[5 + i].astype(F32)
    for j in range(4):
        down[j] = sums[j].astype(F32)
        value = sums[8 + j].astype(F32)
        for i in range(4):
            low = i * width + j * shard
            up[:, low : low + shard] = value[:, i * shard : (i + 1) * shard]


def finish(sums):
    n, rows, width = sums.shape
    tile = 32
    qkv, out, up, down = pl.pallas_call(
        finish_kernel,
        grid=(rows // tile,),
        out_shape=(
            jax.ShapeDtypeStruct((rows, 3 * width), F32),
            jax.ShapeDtypeStruct((rows, width), F32),
            jax.ShapeDtypeStruct((rows, 4 * width), F32),
            jax.ShapeDtypeStruct((4, rows, width), F32),
        ),
        in_specs=[pl.BlockSpec((n, tile, width), lambda i: (0, i, 0))],
        out_specs=(
            pl.BlockSpec((tile, 3 * width), lambda i: (i, 0)),
            pl.BlockSpec((tile, width), lambda i: (i, 0)),
            pl.BlockSpec((tile, 4 * width), lambda i: (i, 0)),
            pl.BlockSpec((4, tile, width), lambda i: (0, i, 0)),
        ),
        compiler_params=pltpu.CompilerParams(dimension_semantics=("arbitrary",), vmem_limit_bytes=32 * 1024 * 1024),
        name="finish",
    )(sums)
    return qkv, out, up, down.reshape(4 * rows, width)


def any_finish(sums):
    shard, width = sums.shape[1:]
    shards, blocks = width // shard, (sums.shape[0] - 4) // 2
    sums = sums.astype(F32)
    up = jnp.transpose(sums[4 : 4 + blocks].reshape(blocks, shard, shards, shard), (1, 2, 0, 3))
    return (
        jnp.transpose(sums[:3], (1, 0, 2)).reshape(shard, 3 * width),
        sums[3],
        up.reshape(shard, blocks * width),
        sums[4 + blocks :].reshape(blocks * shard, width),
    )


def any_gather(w_qkv, w_out, w_up, w_down, small):
    shard, width = w_out.shape
    shards, blocks = width // shard, w_up.shape[1] // width
    up_parts = jnp.transpose(w_up.reshape(shard, shards, blocks, shard), (2, 0, 1, 3)).reshape(blocks, shard, width)
    packed = jnp.concatenate(
        [
            jnp.transpose(w_qkv.reshape(shard, 3, width), (1, 0, 2)),
            w_out[None],
            up_parts,
            w_down.reshape(blocks, shard, width),
        ],
        axis=0,
    )
    return (
        lax.all_gather(packed, "fsdp", axis=1, tiled=True),
        lax.all_gather(small, "fsdp", axis=0, tiled=False),
    )


def any_reduce(parts, small):
    out = []
    for part in parts:
        mine = lax.psum_scatter(part, "fsdp", scatter_dimension=1, tiled=True)
        out.append(lax.psum(mine, "ctx"))
    return jnp.concatenate(out, axis=0), lax.psum(small, ("ctx", "fsdp"))


def any_forward(qkv, lengths):
    count = lengths.shape[0]
    qkv = qkv.reshape(3, count, -1, qkv.shape[2])
    wide = lax.all_to_all(qkv, "ctx", split_axis=3, concat_axis=2, tiled=True)
    wide = jnp.swapaxes(wide, 0, 1)

    def one(item):
        rows, length = item
        mixed, levels = [], []

        def put(start, stop, part, level):
            mixed.append(part)
            levels.append(level)

        attend(rows[0], rows[1], rows[2], length, rows.shape[1], put)
        return mixed[0], levels[0]

    mixed, levels = lax.map(one, (wide, lengths))
    low = lax.all_to_all(mixed.astype(BF16), "ctx", split_axis=1, concat_axis=2, tiled=True)
    return low.reshape(-1, low.shape[2]), wide, mixed, levels


def any_backward(dm_home, wide, mixed, levels, lengths):
    dm_home = dm_home.reshape(lengths.shape[0], -1, dm_home.shape[1])
    dm = lax.all_to_all(dm_home, "ctx", split_axis=2, concat_axis=1, tiled=True)

    def one(item):
        rows, part, level, upstream, length = item
        found = {}

        def put_query(start, stop, value):
            found[0] = value.astype(BF16)

        def put_key(start, stop, d_key, d_value):
            found[1], found[2] = d_key.T.astype(BF16), d_value.T.astype(BF16)

        attend_back(
            rows[0], rows[1], rows[2], part, level, upstream, length, rows.shape[1], put_query, put_key
        )
        return jnp.stack([found[0], found[1], found[2]])

    out = lax.map(one, (wide, mixed, levels, dm, lengths))
    out = lax.all_to_all(out, "ctx", split_axis=2, concat_axis=3, tiled=True)
    out = jnp.swapaxes(out, 0, 1)
    return out.reshape(3, -1, out.shape[3])


def any_layer(w_qkv, w_out, w_up, w_down, small, hidden_in, cotangent, flat_lengths):
    batch, seqs, slots, width = hidden_in.shape
    rows = batch * seqs * slots
    blocks = w_up.shape[1] // width
    weights, small_all = any_gather(w_qkv, w_out, w_up, w_down, small)
    position = lax.axis_index("ctx") * slots + jnp.arange(slots, dtype=jnp.int32)
    filled = (position[None, :] < flat_lengths[:, None]).astype(F32)
    small_all = jnp.transpose(small_all, (1, 0, 2)).reshape(16, width)
    full = small_all.astype(F32)
    full_q, full_v, full_bias_out, gain_one, shift_one, full_bias_down, gain_two, shift_two = [
        full[i] for i in range(8)
    ]
    full_up = small_all[8 : 8 + blocks].reshape(blocks, 1, width)
    flat_in = hidden_in.reshape(rows, width).astype(F32)
    normed = layer_norm(flat_in, gain_one, shift_one).astype(BF16)
    queries = (matmul(normed, weights[0]) + full_q).astype(BF16)
    key_rows = matmul(normed, weights[1]).astype(BF16)
    value_rows = (matmul(normed, weights[2]) + full_v).astype(BF16)
    qkv = jnp.stack([queries, key_rows, value_rows])
    mixed_low, wide, mixed, levels = any_forward(qkv, flat_lengths)
    residual = flat_in + matmul(mixed_low, weights[3]) + full_bias_out
    normed2 = layer_norm(residual, gain_two, shift_two).astype(BF16)
    d_out = cotangent.reshape(rows, width).astype(F32) * filled.reshape(rows, 1)
    fed, d_normed2, grad_up, grad_down, grad_bias_up = feed_forward(
        normed2, d_out.astype(BF16), weights, full_up, 4, 4 + blocks, blocks
    )
    output = (residual + fed + full_bias_down).astype(BF16)
    norm_pull_two = jax.vjp(layer_norm, residual, gain_two, shift_two)[1]
    d_resid_norm, grad_ln2_gain, grad_ln2_bias = norm_pull_two(d_normed2)
    d_residual = d_out + d_resid_norm
    d_attn = d_residual.astype(BF16)
    grad_out = dot_tn(mixed_low, d_attn).astype(BF16)
    d_mixed = dot_nt(d_attn, weights[3]).astype(BF16)
    d_qkv = any_backward(d_mixed, wide, mixed, levels, flat_lengths)
    grad_qkv = jnp.stack([dot_tn(normed, d_qkv[i]).astype(BF16) for i in range(3)])
    d_normed = sum(dot_nt(d_qkv[i], weights[i]) for i in range(3))
    norm_pull_one = jax.vjp(layer_norm, flat_in, gain_one, shift_one)[1]
    d_input_norm, grad_ln1_gain, grad_ln1_bias = norm_pull_one(d_normed)
    small_grads = jnp.stack(
        [
            rows_sum(d_qkv[0]),
            rows_sum(d_qkv[2]),
            rows_sum(d_attn),
            grad_ln1_gain,
            grad_ln1_bias,
            jnp.sum(d_out, axis=0),
            grad_ln2_gain,
            grad_ln2_bias,
        ]
        + [grad_bias_up[j, 0] for j in range(blocks)]
        + [jnp.zeros((width,), F32)] * (8 - blocks)
    )
    return output, d_residual + d_input_norm, [grad_qkv, grad_out[None], grad_up, grad_down], small_grads


def body(
    routed,
    hidden_in,
    lengths,
    cotangent,
    w_qkv,
    bias_q,
    bias_v,
    w_out,
    bias_out,
    ln1_gain,
    ln1_bias,
    w_up,
    bias_up,
    w_down,
    bias_down,
    ln2_gain,
    ln2_bias,
):
    batch, seqs, slots, width = hidden_in.shape
    count = batch * seqs
    rows = count * slots
    shard = w_qkv.shape[0]
    blocks = w_up.shape[1] // width
    vectors = [bias_q, bias_v, bias_out, ln1_gain, ln1_bias, bias_down, ln2_gain, ln2_bias]
    vectors += [bias_up[j * shard : (j + 1) * shard] for j in range(blocks)]
    which = lax.broadcasted_iota(jnp.int32, (16, shard), 0)
    small = jnp.zeros((16, shard), BF16)
    for i, vector in enumerate(vectors):
        small = jnp.where(which == i, vector[None, :], small)
    flat_lengths = lengths.reshape(count)
    if routed:
        *kept, output = forward(
            w_qkv, w_out, w_up, w_down, small,
            hidden_in.reshape(count, slots, width), cotangent.reshape(count, slots, width), lengths,
        )
        sums, small_sums, output, grad_hidden = backward(*kept, output, lengths)
        grad_hidden = grad_hidden.astype(F32)
        out_qkv, out_out, out_up, out_down = finish(sums)
    else:
        output, grad_hidden, parts, small_grads = any_layer(
            w_qkv, w_out, w_up, w_down, small, hidden_in, cotangent, flat_lengths
        )
        sums, small_sums = any_reduce(parts, small_grads)
        out_qkv, out_out, out_up, out_down = any_finish(sums)
    mine = lax.dynamic_slice_in_dim(small_sums, lax.axis_index("fsdp") * shard, shard, 1)
    return (
        output.reshape(hidden_in.shape),
        grad_hidden.reshape(hidden_in.shape),
        out_qkv,
        mine[0],
        mine[1],
        out_out,
        mine[2],
        mine[3],
        mine[4],
        out_up,
        mine[8 : 8 + blocks].reshape(blocks * shard),
        out_down,
        mine[5],
        mine[6],
        mine[7],
    )


def solution(mesh):
    row, vector, slot = P("fsdp", None), P("fsdp"), P(None, "fsdp", "ctx", None)
    routed = dict(mesh.shape) == {"ctx": 8, "fsdp": 4}
    return jax.shard_map(
        functools.partial(body, routed),
        mesh=mesh,
        in_specs=(
            slot, P(None, "fsdp"), slot, row, vector, vector, row, vector, vector, vector, row, vector, row, vector,
            vector, vector,
        ),
        out_specs=(
            slot, slot, row, vector, vector, row, vector, vector, vector, row, vector, row, vector, vector, vector,
        ),
        check_vma=False,
    )
```

time: 545 us -> 298 us (0.55); the launches traced: 537 us -> 297 us
  Pallas kernels: 414 us -> 287 us
  local copies, waits for them, and re-layouts: 74.7 us -> 6.7 us
  other arithmetic: 25.3 us -> 3.07 us
  matrix products: 21.5 us -> 0 us
    pallas_call x5 -> x3, Pallas kernels: 414 us -> 287 us  [the longest x1 146 us: backward(): pl.pallas_call(backward_kernel, out_shape=(shape((n, 2, 2, 2, 2, piece, w...]
    slice x9 -> x2, local copies, waits for them, and re-layouts: 25 us -> 1.68 us  [the longest x1 0.84 us: backward(): small_out[4]]
    dot_general x12 -> x0, matrix products: 21.5 us -> none  [the longest x4 7.88 us: dot_tn(): lax.dot_general(a, b, (((0,), (0,)), ((), ())), preferred_element_type=F32)]
    reshape x7 -> x0, local copies, waits for them, and re-layouts: 19.5 us -> none  [the longest x2 6.89 us: body(): w_up.reshape(shard, shards, blocks, shard)]
    unnamed x78 -> x9, local copies, waits for them, and re-layouts: 15.8 us -> 4.36 us
    transpose x2 -> x0, local copies, waits for them, and re-layouts: 9.68 us -> none  [the longest x1 6.95 us: body(): jnp.transpose(sums[4:4 + blocks].reshape(blocks, shard, shards, shard), (...]
    reduce_sum x9 -> x0, other arithmetic: 7.41 us -> none  [the longest x2 3.52 us: layer_norm(): return centered * lax.rsqrt(spread + EPS) * ln_gain + ln_shift]
where the time goes in v2:
time: 298 us; the launch traced here: 297 us
  Pallas kernels  287 us (96%)
  local copies, waits for them, and re-layouts  6.7 us (2%)
  other arithmetic  3.07 us (1%)
    pallas_call x1, Pallas kernels, backward(): pl.pallas_call(backward_kernel, out_shape=(shape((n, 2, 2, 2, 2, piece, w...  146 us
    pallas_call x1, Pallas kernels, forward(): pl.pallas_call(forward_kernel, out_shape=(shape((4, 4) + piece + (width,)...  135 us

profile of v2, /device:TPU:0, one launch (start us, length us, event | category | flops | bytes accessed | tf_op | source)
XLA Modules:
  0.0 297.2 jit_solution(2054114484700705900)
XLA Ops:
  0.6 0.8 fusion
  1.5 1.5 select_select_fusion.small
  3.0 134.9 %forward.1 = (bf16[4,4,2,2,2,2,16,1024]{7,6,5,4,3,2,1,0:T(8,128)(2,1)}, f32[16,1024]{1,0:T(8,128)}, bf16[4,128,1024]{2,1,0:T(8,128)(2,1)}, bf16[512,1024]{1,0:T(...) custom-call(bf16[2,2,2,2,16,3072]{5,4,3,2,1,0:T(8,128)(2,1)} %bitcas, ...), custom_call_target="tpu_custom_call" | custom-call | tf_op jit(solution)/shard_map/forward/pallas_call | solution.py:561
  137.9 146.4 %backward.1 = (bf16[12,2,2,2,2,16,1024]{6,5,4,3,2,1,0:T(8,128)(2,1)}, f32[5,16,1024]{2,1,0:T(8,128)}, bf16[4,128,1024]{2,1,0:T(8,128)(2,1)}, bf16[4,128,1024]{2,1,0:T(8,128)(2,1)}) custom-call(bf16[4,4,2,2,2,2,16,1024]{7,6,5,4,3,2,1,0:T(8,128)(2,1)} %get-tuple-element.38.kept, f32[16,1024]{1,0:T(8,128)} %get-tuple-element.39.full, ...), custom_call_target="tpu_custom_call" | custom-call | tf_op jit(solution)/shard_map/backward/pallas_call | solution.py:1196
  284.3 0.0 copy-start
  284.3 2.8 copy-done
  287.1 0.0 copy-start.1
  287.1 5.4 %finish.1 = (f32[256,3072]{1,0:T(8,128)}, f32[256,1024]{1,0:T(8,128)}, f32[256,4096]{1,0:T(8,128)}, f32[4,256,1024]{2,1,0:T(8,128)}) custom-call(bf16[12,256,1024]{2,1,0:T(8,128)(2,1)S(1)} %bitcast.26), custom_call_target="tpu_custom_call" | custom-call | tf_op jit(solution)/shard_map/finish/pallas_call | solution.py:1347
  292.5 0.0 copy-start.2
  292.5 0.0 copy-done.1
  292.5 1.6 convert.1
  294.1 0.8 slice.55
  294.9 0.7 constant_dynamic-slice_fusion.7
  295.6 0.6 copy.31
  296.2 0.0 copy-done.2
  296.2 1.0 copy.33
  (7 shorter events, 0.0 us)
Async XLA Ops:
  284.3 2.8 copy-start
  287.1 5.4 %copy-start.1 = (bf16[4,128,1024]{2,1,0:T(8,128)(2,1)S(1)}, bf16[4,128,1024]{2,1,0:T(8,128)(2,1)}, u32[]{:S(2)}) copy-start(bf16[4,128,1024]{2,1,0:T(8,128)(2,1)} %get-tuple-element.54) | copy-start | bytes 3145732
  292.5 3.7 %copy-start.2 = (bf16[4,128,1024]{2,1,0:T(8,128)(2,1)S(1)}, bf16[4,128,1024]{2,1,0:T(8,128)(2,1)}, u32[]{:S(2)}) copy-start(bf16[4,128,1024]{2,1,0:T(8,128)(2,1)} %get-tuple-element.53) | copy-start | bytes 3145732

commit v3 on v2

--- a/solution.py
+++ b/solution.py
@@ -146,8 +146,8 @@
 
 HIDDEN_BLOCKS = 4
 UP, DOWN = 4, 5
-GATHER_OFFSETS = (0, 1, 2, 3, 5, 7, 8)
-GATHER_DELAY = 5
+GATHER_OFFSETS = (0, 1, 2, 3, 6, 8, 9)
+GATHER_DELAY = 4
 
 
 def flat_rows(value):
@@ -385,7 +385,7 @@
         normed[lanes_of(i), :] = part.astype(BF16)
         tick(4 + i)
 
-    @pl.loop(8, 11)
+    @pl.loop(8, 12)
     def _(step):
         tick(step)
 
@@ -404,7 +404,8 @@
                 part += full[u // 2 : u // 2 + 1, cut]
             qkv[u, :, cut] = part.astype(BF16)
 
-        tick(11 + u)
+        if u < 2:
+            tick(12 + u)
 
     def send(h):
         return remote(

time: 298 us -> 297 us (level)
  no operation moved by 1% of the time
where the time goes in v3:
time: 297 us
  Pallas kernels  287 us (97%)
  local copies, waits for them, and re-layouts  6.7 us (2%)
  other arithmetic  3.07 us (1%)
    pallas_call x1, Pallas kernels, backward(): pl.pallas_call(backward_kernel, out_shape=(shape((n, 2, 2, 2, 2, piece, w...  146 us
    pallas_call x1, Pallas kernels, forward(): pl.pallas_call(forward_kernel, out_shape=(shape((4, 4) + piece + (width,)...  135 us

profile of v3, /device:TPU:0, one launch (start us, length us, event | category | flops | bytes accessed | tf_op | source)
XLA Modules:
  0.0 297.0 jit_solution(5371812903335153276)
XLA Ops:
  0.6 0.8 fusion
  1.5 1.5 select_select_fusion.small
  3.0 134.9 %forward.1 = (bf16[4,4,2,2,2,2,16,1024]{7,6,5,4,3,2,1,0:T(8,128)(2,1)}, f32[16,1024]{1,0:T(8,128)}, bf16[4,128,1024]{2,1,0:T(8,128)(2,1)}, bf16[512,1024]{1,0:T(...) custom-call(bf16[2,2,2,2,16,3072]{5,4,3,2,1,0:T(8,128)(2,1)} %bitcas, ...), custom_call_target="tpu_custom_call" | custom-call | tf_op jit(solution)/shard_map/forward/pallas_call | solution.py:562
  137.9 146.2 %backward.1 = (bf16[12,2,2,2,2,16,1024]{6,5,4,3,2,1,0:T(8,128)(2,1)}, f32[5,16,1024]{2,1,0:T(8,128)}, bf16[4,128,1024]{2,1,0:T(8,128)(2,1)}, bf16[4,128,1024]{2,1,0:T(8,128)(2,1)}) custom-call(bf16[4,4,2,2,2,2,16,1024]{7,6,5,4,3,2,1,0:T(8,128)(2,1)} %get-tuple-element.38.kept, f32[16,1024]{1,0:T(8,128)} %get-tuple-element.39.full, ...), custom_call_target="tpu_custom_call" | custom-call | tf_op jit(solution)/shard_map/backward/pallas_call | solution.py:1197
  284.1 0.0 copy-start
  284.2 2.8 copy-done
  286.9 0.0 copy-start.1
  286.9 5.4 %finish.1 = (f32[256,3072]{1,0:T(8,128)}, f32[256,1024]{1,0:T(8,128)}, f32[256,4096]{1,0:T(8,128)}, f32[4,256,1024]{2,1,0:T(8,128)}) custom-call(bf16[12,256,1024]{2,1,0:T(8,128)(2,1)S(1)} %bitcast.26), custom_call_target="tpu_custom_call" | custom-call | tf_op jit(solution)/shard_map/finish/pallas_call | solution.py:1348
  292.4 0.0 copy-start.2
  292.4 0.0 copy-done.1
  292.4 1.6 convert.1
  293.9 0.8 slice.55
  294.8 0.7 constant_dynamic-slice_fusion.7
  295.4 0.6 copy.31
  296.0 0.0 copy-done.2
  296.0 1.0 copy.33
  (7 shorter events, 0.0 us)
Async XLA Ops:
  284.1 2.8 copy-start
  286.9 5.4 %copy-start.1 = (bf16[4,128,1024]{2,1,0:T(8,128)(2,1)S(1)}, bf16[4,128,1024]{2,1,0:T(8,128)(2,1)}, u32[]{:S(2)}) copy-start(bf16[4,128,1024]{2,1,0:T(8,128)(2,1)} %get-tuple-element.54) | copy-start | bytes 3145732
  292.4 3.7 %copy-start.2 = (bf16[4,128,1024]{2,1,0:T(8,128)(2,1)S(1)}, bf16[4,128,1024]{2,1,0:T(8,128)(2,1)}, u32[]{:S(2)}) copy-start(bf16[4,128,1024]{2,1,0:T(8,128)(2,1)} %get-tuple-element.53) | copy-start | bytes 3145732
